TPU v7x, 32 devices: a whole 2x2x4 slice. The times are simulated.
32 devices in a mesh: groups: 2 (over y), ctx: 8 (over z, x), tp: 2 (over core).
Axes of the slice: x: 2, y: 2, z: 4, core: 2. Of those that a mesh axis runs over, the one named last changes fastest.
Arguments:
- tokens: bfloat16 [4096, 2688], P(('groups', 'ctx', 'tp')), parts along dimension 0, may hold values from -6 to 6
- output_gradient: bfloat16 [4096, 2688], P(('groups', 'ctx', 'tp')), parts along dimension 0, may hold values from -6 to 6
- document_index: int32 [4096], P(('groups', 'ctx')), parts along dimension 0, may hold values from 0 to 3, never falling along the last dimension, each value on 1 to 1024 neighbouring positions
- real_token_count: int32 [16], P(('groups', 'ctx')), parts along dimension 0, may hold values from 64 to 256, as said below
- input_norm_gain: float32 [2688], replicated, may hold values from 0.1 to 1.9
- query_norm_gain: float32 [128], replicated, may hold values from 0.1 to 1.9
- key_norm_gain: float32 [128], replicated, may hold values from 0.1 to 1.9
- output_norm_gain: float32 [2688], replicated, may hold values from 0.1 to 1.9
- query_projection: bfloat16 [2688, 512], P(None, 'tp'), may hold values from -0.125 to 0.125
- key_projection: bfloat16 [2688, 256], P(None, 'tp'), may hold values from -0.125 to 0.125
- value_projection: bfloat16 [2688, 256], P(None, 'tp'), may hold values from -0.125 to 0.125
- output_projection: bfloat16 [512, 2688], P('tp'), may hold values from -0.25 to 0.25
- adapter_down_maps: bfloat16 [2688, 48], replicated, may hold values from -0.125 to 0.125
- adapter_query_up: bfloat16 [16, 512], P(None, 'tp'), may hold values from -0.375 to 0.375
- adapter_key_up: bfloat16 [16, 256], P(None, 'tp'), may hold values from -0.375 to 0.375
- adapter_value_up: bfloat16 [16, 256], P(None, 'tp'), may hold values from -0.375 to 0.375
- adapter_output_down: bfloat16 [512, 16], P('tp'), may hold values from -0.25 to 0.25
- adapter_output_up: bfloat16 [16, 2688], replicated, may hold values from -0.375 to 0.375
Outputs:
- layer_out: bfloat16 [4096, 2688], P(('groups', 'ctx', 'tp')), parts along dimension 0
- grad_in: bfloat16 [4096, 2688], P(('groups', 'ctx', 'tp')), parts along dimension 0
- grad_down: float32 [5376, 48], P(('groups', 'tp')), parts along dimension 0
- query_up_gradient: float32 [32, 512], P('groups', 'tp'), parts along dimension 0
- key_up_gradient: float32 [32, 256], P('groups', 'tp'), parts along dimension 0
- value_up_gradient: float32 [32, 256], P('groups', 'tp'), parts along dimension 0
- grad_down_out: float32 [1024, 16], P(('groups', 'tp')), parts along dimension 0
- output_up_gradient: float32 [32, 2688], P('groups', 'tp'), parts along dimension 0
There are 2 independent parts, one for each index of `groups`. A program takes and returns all parts, laid end to end along the dimension named above; an argument that names none is the same for every part. Nothing has to cross between parts.
Inputs may be any that keep to these rules, and one draw needn't show every extreme that they name: `document_index`: document numbers never fall along the tokens; a document has 1 to 1024 tokens and one has exactly that many. `real_token_count`: the real tokens of a block come first and the rest is padding; some block is full and some holds 64 real tokens.
All inputs are finite; a program needn't handle non-finite values.
Results may differ from a plain program's by a relative error of at most 0.034.
Values may be sent and summed in bfloat16 or wider, within the bound.
A program may use at most 64 MiB of HBM per device.

v0:
```python
import jax
import jax.numpy as jnp
from jax import lax
from jax.sharding import PartitionSpec as P

WINDOW = 1024


epsilon = 1e-06
adapter_scale = 2.0
score_scale = 168.0 ** (-0.5)


def passed_along(value, axis, steps):
    count = lax.axis_size(axis)
    leading, last = (max(0, -steps), min(count, count - steps))
    return lax.ppermute(value, axis, [(source, source + steps) for source in range(leading, last)])


def norm_rows(source, gain_vec):
    inverse = lax.rsqrt(jnp.mean(source * source, axis=-1, keepdims=True) + epsilon)
    return source * inverse * gain_vec


def norm_back(source, gain_vec, incoming):
    inverse = lax.rsqrt(jnp.mean(source * source, axis=-1, keepdims=True) + epsilon)
    scaled = source * inverse
    upward = incoming * gain_vec
    return inverse * (upward - scaled * jnp.mean(upward * scaled, axis=-1, keepdims=True))


def matrix_product(first_op, second_op):
    return jnp.dot(first_op, second_op, preferred_element_type=jnp.float32)


def multiply_by_transpose(first_op, second_op):
    return lax.dot_general(
        first_op, second_op, (((1,), (1,)), ((), ())), preferred_element_type=jnp.float32
    )


def transpose_multiply(first_op, second_op):
    return lax.dot_general(
        first_op, second_op, (((0,), (0,)), ((), ())), preferred_element_type=jnp.float32
    )


def window_mask(query_segs, key_codes):
    query_count = query_segs.shape[0]
    key_total = key_codes.shape[0]
    distance = (key_total - query_count + jnp.arange(query_count))[:, None] - jnp.arange(key_total)[
        None, :
    ]
    same_doc = key_codes[None, :] == query_segs[:, None] + 1
    return (distance == 0) | (distance > 0) & (distance < WINDOW) & same_doc


def on_device(
    tokens,
    output_gradient,
    document_index,
    real_token_count,
    input_norm_gain,
    query_norm_gain,
    key_norm_gain,
    output_norm_gain,
    query_projection,
    key_projection,
    value_projection,
    output_projection,
    adapter_down_maps,
    adapter_query_up,
    adapter_key_up,
    adapter_value_up,
    adapter_output_down,
    adapter_output_up,
):
    row_count, model_width = tokens.shape
    shard_len = document_index.shape[0]
    head_dim = key_projection.shape[1]
    adapter_product = adapter_key_up.shape[0]
    heads_here = query_projection.shape[1] // head_dim
    ctx_size = lax.axis_size("ctx")
    tp_index = lax.axis_index("tp")
    slice_width = model_width // lax.axis_size("tp")
    reach_shards = WINDOW // shard_len
    send_count = min(reach_shards, ctx_size - 1)
    tok_float = tokens.astype(jnp.float32)
    normed_rows = norm_rows(tok_float, input_norm_gain).astype(jnp.bfloat16)
    normalized_input = lax.all_gather(normed_rows, "tp", axis=0, tiled=True)
    middle_list = matrix_product(normalized_input, adapter_down_maps).astype(jnp.bfloat16)
    middle_query = middle_list[:, :adapter_product]
    middle_key = middle_list[:, adapter_product : 2 * adapter_product]
    middle_value = middle_list[:, 2 * adapter_product :]
    query_before_norm = matrix_product(
        normalized_input, query_projection
    ) + adapter_scale * matrix_product(middle_query, adapter_query_up)
    key_before_norm = matrix_product(
        normalized_input, key_projection
    ) + adapter_scale * matrix_product(middle_key, adapter_key_up)
    value_before_norm = matrix_product(
        normalized_input, value_projection
    ) + adapter_scale * matrix_product(middle_value, adapter_value_up)
    query_heads = query_before_norm.reshape(shard_len, heads_here, head_dim)
    query_normed = norm_rows(query_heads, query_norm_gain).astype(jnp.bfloat16)
    key_normed = norm_rows(key_before_norm, key_norm_gain).astype(jnp.bfloat16)
    value_cast = value_before_norm.astype(jnp.bfloat16)
    positions = jnp.arange(shard_len)
    is_valid = positions < real_token_count[0]
    valid_rows = is_valid.astype(jnp.float32)
    local_codes = jnp.where(is_valid, document_index + 1, 0)
    local_pair = jnp.concatenate([key_normed, value_cast], axis=1)
    received = []
    for hop_index in range(1, send_count + 1):
        received.append(passed_along((local_pair, local_codes), "ctx", hop_index))
    missing = reach_shards - send_count
    blank_pair = jnp.zeros_like(local_pair)
    blank_codes = jnp.zeros_like(local_codes)
    earlier = [(blank_pair, blank_codes)] * missing + list(reversed(received))
    key_pairs = jnp.concatenate([entry[0] for entry in earlier] + [local_pair], axis=0)
    key_codes_all = jnp.concatenate([entry[1] for entry in earlier] + [local_codes], axis=0)
    keys_all = key_pairs[:, :head_dim]
    values_all = key_pairs[:, head_dim:]
    allowed = window_mask(document_index, key_codes_all)
    scores = (
        jnp.einsum("thd,sd->hts", query_normed, keys_all, preferred_element_type=jnp.float32)
        * score_scale
    )
    weights = jnp.where(allowed[None], jnp.exp(scores), 0.0)
    attn_probs = weights / jnp.sum(weights, axis=-1, keepdims=True)
    probs_cast = attn_probs.astype(jnp.bfloat16)
    attention_result = jnp.einsum(
        "hts,sd->thd", probs_cast, values_all, preferred_element_type=jnp.float32
    )
    attention_result = (
        (attention_result * valid_rows[:, None, None])
        .astype(jnp.bfloat16)
        .reshape(shard_len, heads_here * head_dim)
    )
    part_out = matrix_product(attention_result, output_projection)
    partial_middle = matrix_product(attention_result, adapter_output_down)
    output_total, mid_sum = (
        lax.psum_scatter(
            part_out.astype(jnp.bfloat16), "tp", scatter_dimension=0, tiled=True
        ).astype(jnp.float32),
        lax.psum_scatter(
            partial_middle.astype(jnp.bfloat16), "tp", scatter_dimension=0, tiled=True
        ).astype(jnp.float32),
    )
    middle_output = mid_sum.astype(jnp.bfloat16)
    apply_prenorm = output_total + adapter_scale * matrix_product(middle_output, adapter_output_up)
    layer_out = norm_rows(apply_prenorm, output_norm_gain).astype(jnp.bfloat16)
    prenorm_gradient = norm_back(
        apply_prenorm, output_norm_gain, output_gradient.astype(jnp.float32)
    ).astype(jnp.bfloat16)
    middle_output_gradient = (
        adapter_scale * multiply_by_transpose(prenorm_gradient, adapter_output_up)
    ).astype(jnp.bfloat16)
    complete_gradient, middle_complete_gradient, middle_complete = (
        lax.all_gather(prenorm_gradient, "tp", axis=0, tiled=True),
        lax.all_gather(middle_output_gradient, "tp", axis=0, tiled=True),
        lax.all_gather(middle_output, "tp", axis=0, tiled=True),
    )
    gradient_portion = lax.dynamic_slice_in_dim(
        complete_gradient, tp_index * slice_width, slice_width, 1
    )
    output_up_contribution = adapter_scale * transpose_multiply(middle_complete, gradient_portion)
    attention_gradient = multiply_by_transpose(
        complete_gradient, output_projection
    ) + multiply_by_transpose(middle_complete_gradient, adapter_output_down)
    attention_gradient = (attention_gradient * valid_rows[:, None]).astype(jnp.bfloat16)
    down_out_term = transpose_multiply(attention_result, middle_complete_gradient)
    grad_heads = attention_gradient.reshape(shard_len, heads_here, head_dim)
    grad_probs = jnp.einsum(
        "thd,sd->hts", grad_heads, values_all, preferred_element_type=jnp.float32
    )
    inner_sum = jnp.sum(attn_probs * grad_probs, axis=-1, keepdims=True)
    grad_scores = (attn_probs * (grad_probs - inner_sum) * score_scale).astype(jnp.bfloat16)
    grad_query = jnp.einsum(
        "hts,sd->thd", grad_scores, keys_all, preferred_element_type=jnp.float32
    )
    grad_keys = jnp.einsum(
        "hts,thd->sd", grad_scores, query_normed, preferred_element_type=jnp.float32
    )
    grad_values = jnp.einsum(
        "hts,thd->sd", probs_cast, grad_heads, preferred_element_type=jnp.float32
    )
    grad_pairs = jnp.concatenate([grad_keys, grad_values], axis=1)
    own_grads = grad_pairs[reach_shards * shard_len :]
    for hop_index in range(1, send_count + 1):
        own_grads = own_grads + passed_along(
            grad_pairs[
                (reach_shards - hop_index) * shard_len : (reach_shards - hop_index + 1) * shard_len
            ].astype(jnp.bfloat16),
            "ctx",
            -hop_index,
        ).astype(jnp.float32)
    query_prenorm_gradient = (
        norm_back(query_heads, query_norm_gain, grad_query)
        .reshape(shard_len, heads_here * head_dim)
        .astype(jnp.bfloat16)
    )
    key_prenorm_gradient = norm_back(
        key_before_norm, key_norm_gain, own_grads[:, :head_dim]
    ).astype(jnp.bfloat16)
    value_prenorm_gradient = own_grads[:, head_dim:].astype(jnp.bfloat16)
    query_up_contribution = adapter_scale * transpose_multiply(middle_query, query_prenorm_gradient)
    key_up_contribution = adapter_scale * transpose_multiply(middle_key, key_prenorm_gradient)
    value_up_contribution = adapter_scale * transpose_multiply(middle_value, value_prenorm_gradient)
    middle_gradients = jnp.concatenate(
        [
            adapter_scale * multiply_by_transpose(query_prenorm_gradient, adapter_query_up),
            adapter_scale * multiply_by_transpose(key_prenorm_gradient, adapter_key_up),
            adapter_scale * multiply_by_transpose(value_prenorm_gradient, adapter_value_up),
        ],
        axis=1,
    ).astype(jnp.bfloat16)
    grad_normed = (
        multiply_by_transpose(query_prenorm_gradient, query_projection)
        + multiply_by_transpose(key_prenorm_gradient, key_projection)
        + multiply_by_transpose(value_prenorm_gradient, value_projection)
        + multiply_by_transpose(middle_gradients, adapter_down_maps)
    )
    grad_normed_rows = lax.psum_scatter(
        grad_normed.astype(jnp.bfloat16), "tp", scatter_dimension=0, tiled=True
    ).astype(jnp.float32)
    grad_in = norm_back(tok_float, input_norm_gain, grad_normed_rows).astype(jnp.bfloat16)
    down_term = lax.psum_scatter(
        transpose_multiply(normalized_input, middle_gradients).astype(jnp.bfloat16),
        "tp",
        scatter_dimension=0,
        tiled=True,
    )
    adapter_totals = (
        lax.psum(down_term, "ctx").astype(jnp.float32),
        lax.psum(query_up_contribution.astype(jnp.bfloat16), "ctx").astype(jnp.float32),
        lax.psum(key_up_contribution.astype(jnp.bfloat16), "ctx").astype(jnp.float32),
        lax.psum(value_up_contribution.astype(jnp.bfloat16), "ctx").astype(jnp.float32),
        lax.psum(down_out_term.astype(jnp.bfloat16), "ctx").astype(jnp.float32),
        lax.psum(output_up_contribution.astype(jnp.bfloat16), "ctx").astype(jnp.float32),
    )
    return (
        layer_out,
        grad_in,
        adapter_totals[0],
        adapter_totals[1],
        adapter_totals[2],
        adapter_totals[3],
        adapter_totals[4],
        adapter_totals[5],
    )


def solution(mesh):
    in_specs = (
        P(("groups", "ctx", "tp"), None),
        P(("groups", "ctx", "tp"), None),
        P(("groups", "ctx")),
        P(("groups", "ctx")),
        P(),
        P(),
        P(),
        P(),
        P(None, "tp"),
        P(None, "tp"),
        P(None, "tp"),
        P("tp", None),
        P(),
        P(None, "tp"),
        P(None, "tp"),
        P(None, "tp"),
        P("tp", None),
        P(),
    )
    out_specs = (
        P(("groups", "ctx", "tp"), None),
        P(("groups", "ctx", "tp"), None),
        P(("groups", "tp"), None),
        P("groups", "tp"),
        P("groups", "tp"),
        P("groups", "tp"),
        P(("groups", "tp"), None),
        P("groups", "tp"),
    )
    return jax.shard_map(
        on_device, mesh=mesh, in_specs=in_specs, out_specs=out_specs, check_vma=False
    )
```

profile of v0, /device:TPU:0, one launch (start us, length us, event | category | flops | bytes accessed | tf_op | source)
XLA Modules:
  0.0 319.8 jit_solution(16461796081767223556)
XLA Ops:
  7.2 1.4 fusion.26
  9.2 2.2 fusion.21
  12.2 5.9 %collective-permute-start.4 = (s32[256]{0:T(256)S(1)}, s32[256]{0:T(256)S(1)}, u32[]{:S(2)}, u32[]{:S(2)}) collective-permute-start(s32[256]{0:T(256)S(1)} %get-tuple-element.19), channel_id=1, source_target_pairs={{0,8},{2,10},{4,12},{6,14},{1,9},{3,11},{5,13},{7,15},{16,24},{18,... | collective-permute-start | bytes 3080 | tf_op jit(solution)/shard_map/ppermute | solution.py:17
  18.1 4.4 %collective-permute-start.5 = (s32[256]{0:T(256)S(1)}, s32[256]{0:T(256)S(1)}, u32[]{:S(2)}, u32[]{:S(2)}) collective-permute-start(s32[256]{0:T(256)S(1)} %get-tuple-element.19), channel_id=1, source_target_pairs={{0,6},{2,8},{4,10},{6,12},{8,14},{1,7},{3,9},{5,11},{7,13},{9,15},... | collective-permute-start | bytes 3080 | tf_op jit(solution)/shard_map/ppermute | solution.py:17
  23.8 3.1 collective-permute-start.7
  28.2 1.3 fusion.35
  29.5 2.0 convolution_convert_fusion.2
  33.5 3.9 %collective-permute-start = (bf16[256,256]{0,1:T(8,128)(2,1)S(1)}, bf16[256,256]{0,1:T(8,128)(2,1)S(1)}, u32[]{:S(2)}, u32[]{:S(2)}) collective-permute-start(bf16[256,256]{0,1:T(8,128)(2,1)S(1)} %pad_maximum_fusion.1), channel_id=1, source_target_pairs={{0,8},{2,10},{4,12},{6,14},{1,9},{3,11},{5,13},{7,15},{16,24},{18,... | collective-permute-start | bytes 393224 | tf_op jit(solution)/shard_map/ppermute | solution.py:17
  37.4 1.3 collective-permute-start.1
  38.7 1.9 collective-permute-start.2
  40.5 2.8 collective-permute-start.3
  47.9 3.4 %fusion.31 = f32[2,256,1280]{1,2,0:T(8,128)} fusion(pred[256,1280]{0,1:T(8,128)(4,1)S(1)} %copy-done.21, bf16[1280,256]{0,1:T(8,128)(2,1)} %constant_dynamic-update-slice_fusion, f32[256,256]{0,1:T(8,128)S(1)} %get-tuple-element.24, f32[128]{0:T(128)S(1)} %copy-done.43, f32[256,2]{0,1:T(2,128)S(1)} %add_rsqrt_fusion), kind=kOutput, calls=%fused_computation.49 | convolution fusion | flops 169936640 | bytes 3541504 | tf_op jit(solution)/shard_map/div | solution.py:130
  51.3 2.2 fusion.46
  54.5 3.0 convolution_convert_fusion
  57.6 8.8 %reduce-scatter.13.cloned.1.call-done = bf16[128,16]{1,0:T(8,128)(2,1)} async-done(((bf16[256,16]{1,0:T(8,128)(2,1)}), bf16[128,16]{1,0:T(8,128)(2,1)}) %reduce-scatter.13.cloned.1.call-update) | async-done | bytes 4112
  66.4 12.3 %reduce-scatter.9.cloned.1.call-done = bf16[128,2688]{1,0:T(8,128)(2,1)} async-done(((bf16[256,2688]{1,0:T(8,128)(2,1)}), bf16[128,2688]{1,0:T(8,128)(2,1)}) %reduce-scatter.9.cloned.1.call-update) | async-done | bytes 688144 | tf_op jit(solution)/shard_map/reduce_scatter | solution.py:143
  78.6 1.6 multiply_reduce_fusion.2
  80.6 1.5 multiply_convert_fusion
  83.1 1.8 all_gather.15
  84.9 1.4 fusion.52
  86.2 1.9 all_gather.14
  89.1 4.0 %all-gather.5.cloned.1.call-done = bf16[256,2688]{1,0:T(8,128)(2,1)} async-done(((bf16[128,2688]{1,0:T(8,128)(2,1)}), bf16[256,2688]{1,0:T(8,128)(2,1)}) %all-gather.5.cloned.1.call-update) | async-done | bytes 1376272 | tf_op jit(solution)/shard_map/all_gather | solution.py:160
  93.1 2.3 fusion.45
  95.4 3.2 convolution_bitcast_fusion
  99.3 5.7 %multiply_reduce_fusion.3 = (f32[256,2]{0,1:T(2,128)S(1)}, f32[256,2,128]{0,2,1:T(8,128)}) fusion(f32[256,256]{0,1:T(8,128)} %copy-done.18, f32[256,2]{0,1:T(2,128)S(1)} %copy-done.37, f32[128]{0:T(128)S(1)} %copy-done.44, f32[2,256,1280]{1,2,0:T(8,128)} %fusion.31, f32[2,256,1280]{1,2,0:T(8,128)} %convolution_bitcast_fusion, ...), kind=kOutput, calls=%fused_computation.99 | convolution fusion | flops 171312384 | bytes 11342336 | tf_op jit(solution)/shard_map/hts,sd->thd/dot_general | solution.py:179
  105.0 5.7 %convolution_bitcast_fusion.2 = f32[1280,128]{0,1:T(8,128)} fusion(f32[2,256,1280]{1,2,0:T(8,128)} %fusion.31, f32[2,256,1280]{1,2,0:T(8,128)} %convolution_bitcast_fusion, f32[256,256]{0,1:T(8,128)} %copy-done.18, f32[128]{0:T(128)S(1)} %copy-done.44, f32[256,2]{0,1:T(2,128)S(1)} %copy-done.37), kind=kOutput, calls=%fused_computation.19 | convolution fusion | flops 171247360 | bytes 6162944 | tf_op jit(solution)/shard_map/hts,thd->sd/dot_general | solution.py:182
  112.7 2.1 fusion.83
  115.0 1.4 collective-permute-start.10
  116.4 1.3 collective-permute-start.11
  117.7 1.3 collective-permute-start.8
  119.0 1.6 collective-permute-start.9
  121.7 2.0 collective-permute-done.10
  123.7 10.1 %collective-permute-done.11 = bf16[256,256]{0,1:T(8,128)(2,1)S(1)} collective-permute-done((bf16[256,256]{0,1:T(8,128)(2,1)S(1)}, bf16[256,256]{0,1:T(8,128)(2,1)S(1)}, u32[]{:S(2)}, u32[]{:S(2)}) %collective-permute-start.11) | collective-permute-done | bytes 131104 | tf_op jit(solution)/shard_map/ppermute | solution.py:17
  136.9 2.1 copy.54
  139.8 3.9 %convolution_add_fusion.1 = f32[256,2688]{1,0:T(8,128)} fusion(f32[256,2688]{1,0:T(8,128)} %fusion.83, bf16[256,128]{0,1:T(8,128)(2,1)S(1)} %multiply_convert_fusion.4, bf16[2688,128]{1,0:T(8,128)(2,1)S(1)} %copy-done.8), kind=kOutput, calls=%fused_computation.2 | convolution fusion | flops 176848896 | bytes 6258688 | tf_op jit(solution)/shard_map/dot_general | solution.py:37
  143.8 2.1 fusion.63
  145.9 3.6 %reduce-scatter.15.cloned.1.call-done = bf16[1344,48]{1,0:T(8,128)(2,1)} async-done(((bf16[2688,48]{1,0:T(8,128)(2,1)}), bf16[1344,48]{1,0:T(8,128)(2,1)}) %reduce-scatter.15.cloned.1.call-update) | async-done | bytes 129040
  149.5 1.8 copy.55
  151.4 4.3 %fusion.2 = bf16[256,2688]{1,0:T(8,128)(2,1)} fusion(f32[256,2688]{1,0:T(8,128)} %fusion.63, f32[256,2688]{1,0:T(8,128)} %convolution_add_fusion.1, bf16[2688,128]{1,0:T(8,128)(2,1)S(1)} %copy-done.12, f32[256,256]{0,1:T(8,128)S(1)} %copy-done.5), kind=kOutput, calls=%fused_computation.5 | convolution fusion | flops 178225152 | bytes 7634944 | tf_op jit(solution)/shard_map/dot_general | solution.py:37
  155.7 70.0 %all-reduce.6.cloned.1.call-done = (bf16[16,256]{1,0:T(8,128)(2,1)}, bf16[16,128]{1,0:T(8,128)(2,1)}, bf16[16,128]{1,0:T(8,128)(2,1)}, bf16[256,16]{0,1:T(8,128)(2,1)}, bf16[16,1344]{1,0:T(8,128)(2,1)}) async-done(((bf16[16,256]{1,0:T(8,128)(2,1)}, bf16[16,128]{1,0:T(8,128)(2,1)}, bf16[16,128]{1,0:T(8,128)(2,1)}, bf16[256,16]{0,1:T(8,128)(2,1)}, bf16[16,1344]{1,0:T(8,128)(2,1)}), ...) | async-done | bytes 67600 | tf_op jit(solution)/shard_map/psum | solution.py:236
  225.7 1.4 convert_element_type.179
  227.1 1.3 convert_element_type.171
  228.4 1.3 convert_element_type.177
  232.3 67.5 %all-reduce.4.cloned.1.call-done = bf16[1344,48]{0,1:T(8,128)(2,1)} async-done(((bf16[1344,48]{0,1:T(8,128)(2,1)}), bf16[1344,48]{0,1:T(8,128)(2,1)}) %all-reduce.4.cloned.1.call-update) | async-done | bytes 129040 | tf_op jit(solution)/shard_map/psum | solution.py:235
  299.8 1.6 convert_element_type.169
  301.4 8.7 %reduce-scatter.11.cloned.1.call-done = bf16[128,2688]{1,0:T(8,128)(2,1)} async-done(((bf16[256,2688]{1,0:T(8,128)(2,1)}), bf16[128,2688]{1,0:T(8,128)(2,1)}) %reduce-scatter.11.cloned.1.call-update) | async-done | bytes 688144 | tf_op jit(solution)/shard_map/reduce_scatter | solution.py:224
  310.1 1.6 fusion.22
  311.7 1.3 fusion.25
  (171 shorter events, 23.1 us)
Async XLA Ops:
  7.2 36.4 %copy-start = (bf16[2688,256]{1,0:T(8,128)(2,1)S(1)}, bf16[2688,256]{1,0:T(8,128)(2,1)}, u32[]{:S(2)}) copy-start(bf16[2688,256]{1,0:T(8,128)(2,1)} %param.26) | copy-start | bytes 4128772
  7.2 5.0 %copy-start.42 = (s32[256]{0:T(256)S(1)}, s32[256]{0:T(256)}, u32[]{:S(2)}) copy-start(s32[256]{0:T(256)} %param.20) | copy-start | bytes 3076
  7.2 22.3 %all-gather.3.cloned.1.call-start = ((), (), s32[]{:S(2)}) async-start(), calls=%async_computation.4 | async-start | bytes 2064384 | tf_op jit(solution)/shard_map/all_gather | solution.py:90
  11.4 20.2 %copy-start.32 = (bf16[16,128]{1,0:T(8,128)(2,1)S(1)}, bf16[16,128]{1,0:T(8,128)(2,1)}, u32[]{:S(2)}) copy-start(bf16[16,128]{1,0:T(8,128)(2,1)} %param.32) | copy-start | bytes 12292
  11.4 20.4 %copy-start.7 = (bf16[2688,128]{1,0:T(8,128)(2,1)S(1)}, bf16[2688,128]{1,0:T(8,128)(2,1)}, u32[]{:S(2)}) copy-start(bf16[2688,128]{1,0:T(8,128)(2,1)} %param.27) | copy-start | bytes 2064388
  11.4 55.0 %reduce-scatter.13.cloned.1.call-start = ((), (), s32[]{:S(2)}) async-start(), calls=%async_computation.9 | async-start | bytes 98304
  12.2 14.8 %collective-permute-start.4 = (s32[256]{0:T(256)S(1)}, s32[256]{0:T(256)S(1)}, u32[]{:S(2)}, u32[]{:S(2)}) collective-permute-start(s32[256]{0:T(256)S(1)} %get-tuple-element.19), channel_id=1, source_target_pairs={{0,8},{2,10},{4,12},{6,14},{1,9},{3,11},{5,13},{7,15},{16,24},{18,... | collective-permute-start | bytes 3080 | tf_op jit(solution)/shard_map/ppermute | solution.py:17
  18.1 8.9 %collective-permute-start.5 = (s32[256]{0:T(256)S(1)}, s32[256]{0:T(256)S(1)}, u32[]{:S(2)}, u32[]{:S(2)}) collective-permute-start(s32[256]{0:T(256)S(1)} %get-tuple-element.19), channel_id=1, source_target_pairs={{0,6},{2,8},{4,10},{6,12},{8,14},{1,7},{3,9},{5,11},{7,13},{9,15},... | collective-permute-start | bytes 3080 | tf_op jit(solution)/shard_map/ppermute | solution.py:17
  22.5 4.5 %collective-permute-start.6 = (s32[256]{0:T(256)S(1)}, s32[256]{0:T(256)S(1)}, u32[]{:S(2)}, u32[]{:S(2)}) collective-permute-start(s32[256]{0:T(256)S(1)} %get-tuple-element.19), channel_id=1, source_target_pairs={{0,4},{2,6},{4,8},{6,10},{8,12},{10,14},{1,5},{3,7},{5,9},{7,11},{... | collective-permute-start | bytes 3080 | tf_op jit(solution)/shard_map/ppermute | solution.py:17
  23.8 4.4 %collective-permute-start.7 = (s32[256]{0:T(256)S(1)}, s32[256]{0:T(256)S(1)}, u32[]{:S(2)}, u32[]{:S(2)}) collective-permute-start(s32[256]{0:T(256)S(1)} %get-tuple-element.19), channel_id=1, source_target_pairs={{0,2},{2,4},{4,6},{6,8},{8,10},{10,12},{12,14},{1,3},{3,5},{5,7},{... | collective-permute-start | bytes 3080 | tf_op jit(solution)/shard_map/ppermute | solution.py:17
  27.0 24.3 %copy-start.34 = (f32[256]{0:T(256)}, f32[256]{0:T(256)S(1)}, u32[]{:S(2)}) copy-start(f32[256]{0:T(256)S(1)} %fusion.70) | copy-start | bytes 3076
  32.7 10.7 %copy-start.28 = (bf16[16,256]{1,0:T(8,128)(2,1)S(1)}, bf16[16,256]{1,0:T(8,128)(2,1)}, u32[]{:S(2)}) copy-start(bf16[16,256]{1,0:T(8,128)(2,1)} %param.31) | copy-start | bytes 24580
  33.5 10.9 %collective-permute-start = (bf16[256,256]{0,1:T(8,128)(2,1)S(1)}, bf16[256,256]{0,1:T(8,128)(2,1)S(1)}, u32[]{:S(2)}, u32[]{:S(2)}) collective-permute-start(bf16[256,256]{0,1:T(8,128)(2,1)S(1)} %pad_maximum_fusion.1), channel_id=1, source_target_pairs={{0,8},{2,10},{4,12},{6,14},{1,9},{3,11},{5,13},{7,15},{16,24},{18,... | collective-permute-start | bytes 393224 | tf_op jit(solution)/shard_map/ppermute | solution.py:17
  37.4 7.7 %collective-permute-start.1 = (bf16[256,256]{0,1:T(8,128)(2,1)S(1)}, bf16[256,256]{0,1:T(8,128)(2,1)S(1)}, u32[]{:S(2)}, u32[]{:S(2)}) collective-permute-start(bf16[256,256]{0,1:T(8,128)(2,1)S(1)} %pad_maximum_fusion.1), channel_id=1, source_target_pairs={{0,6},{2,8},{4,10},{6,12},{8,14},{1,7},{3,9},{5,11},{7,13},{9,15},... | collective-permute-start | bytes 393224 | tf_op jit(solution)/shard_map/ppermute | solution.py:17
  38.7 7.1 %collective-permute-start.2 = (bf16[256,256]{0,1:T(8,128)(2,1)S(1)}, bf16[256,256]{0,1:T(8,128)(2,1)S(1)}, u32[]{:S(2)}, u32[]{:S(2)}) collective-permute-start(bf16[256,256]{0,1:T(8,128)(2,1)S(1)} %pad_maximum_fusion.1), channel_id=1, source_target_pairs={{0,4},{2,6},{4,8},{6,10},{8,12},{10,14},{1,5},{3,7},{5,9},{7,11},{... | collective-permute-start | bytes 393224 | tf_op jit(solution)/shard_map/ppermute | solution.py:17
  40.5 5.9 %collective-permute-start.3 = (bf16[256,256]{0,1:T(8,128)(2,1)S(1)}, bf16[256,256]{0,1:T(8,128)(2,1)S(1)}, u32[]{:S(2)}, u32[]{:S(2)}) collective-permute-start(bf16[256,256]{0,1:T(8,128)(2,1)S(1)} %pad_maximum_fusion.1), channel_id=1, source_target_pairs={{0,2},{2,4},{4,6},{6,8},{8,10},{10,12},{12,14},{1,3},{3,5},{5,7},{... | collective-permute-start | bytes 393224 | tf_op jit(solution)/shard_map/ppermute | solution.py:17
  43.6 4.3 %copy-start.21 = (pred[256,1280]{0,1:T(8,128)(4,1)S(1)}, pred[256,1280]{0,1:T(8,128)(4,1)}, u32[]{:S(2)}) copy-start(pred[256,1280]{0,1:T(8,128)(4,1)} %fusion.35) | copy-start | bytes 983044
  43.6 4.2 %copy-start.43 = (f32[128]{0:T(128)S(1)}, f32[128]{0:T(128)}, u32[]{:S(2)}) copy-start(f32[128]{0:T(128)} %param.23) | copy-start | bytes 1540
  44.3 6.9 %copy-start.36 = (f32[256,2]{0,1:T(2,128)}, f32[256,2]{0,1:T(2,128)S(1)}, u32[]{:S(2)}) copy-start(f32[256,2]{0,1:T(2,128)S(1)} %add_rsqrt_fusion) | copy-start | bytes 6148
  53.5 4.0 %copy-start.16 = (bf16[128,2,256]{2,0,1:T(8,128)(2,1)}, bf16[128,2,256]{2,0,1:T(8,128)(2,1)S(1)}, u32[]{:S(2)}) copy-start(bf16[128,2,256]{2,0,1:T(8,128)(2,1)S(1)} %fusion.46) | copy-start | bytes 393220
  54.4 24.2 %reduce-scatter.9.cloned.1.call-start = ((), (), s32[]{:S(2)}) async-start(), calls=%async_computation.5 | async-start | bytes 2064384 | tf_op jit(solution)/shard_map/reduce_scatter | solution.py:143
  57.5 21.2 %copy-start.20 = (bf16[16,2688]{1,0:T(8,128)(2,1)S(1)}, bf16[16,2688]{1,0:T(8,128)(2,1)}, u32[]{:S(2)}) copy-start(bf16[16,2688]{1,0:T(8,128)(2,1)} %param.35) | copy-start | bytes 258052
  57.5 22.7 %copy-start.9 = (bf16[128,2688]{1,0:T(8,128)(2,1)S(1)}, bf16[128,2688]{1,0:T(8,128)(2,1)}, u32[]{:S(2)}) copy-start(bf16[128,2688]{1,0:T(8,128)(2,1)} %param.19) | copy-start | bytes 2064388
  57.5 35.6 %all-gather.5.cloned.1.call-start = ((), (), s32[]{:S(2)}) async-start(), calls=%async_computation.6 | async-start | bytes 2064384 | tf_op jit(solution)/shard_map/all_gather | solution.py:160
  82.1 5.9 %copy-start.17 = (bf16[128,2,256]{2,0,1:T(8,128)(2,1)S(1)}, bf16[128,2,256]{2,0,1:T(8,128)(2,1)}, u32[]{:S(2)}) copy-start(bf16[128,2,256]{2,0,1:T(8,128)(2,1)} %copy-done.16) | copy-start | bytes 393220
  82.1 6.7 %copy-start.27 = (bf16[256,16]{0,1:T(8,128)(2,1)S(1)}, bf16[256,16]{0,1:T(8,128)(2,1)}, u32[]{:S(2)}) copy-start(bf16[256,16]{0,1:T(8,128)(2,1)} %param.34) | copy-start | bytes 24580
  82.1 10.9 %copy-start.35 = (f32[256]{0:T(256)S(1)}, f32[256]{0:T(256)}, u32[]{:S(2)}) copy-start(f32[256]{0:T(256)} %copy-done.34) | copy-start | bytes 3076
  82.2 67.3 %reduce-scatter.15.cloned.1.call-start = ((), (), s32[]{:S(2)}) async-start(), calls=%async_computation.10 | async-start | bytes 1032192
  105.0 7.6 %copy-start.29 = (bf16[16,256]{1,0:T(8,128)(2,1)S(1)}, bf16[16,256]{1,0:T(8,128)(2,1)}, u32[]{:S(2)}) copy-start(bf16[16,256]{1,0:T(8,128)(2,1)} %param.31) | copy-start | bytes 24580
  114.8 5.8 %copy-start.6 = (bf16[256,2688]{1,0:T(8,128)(2,1)S(1)}, bf16[256,2688]{1,0:T(8,128)(2,1)}, u32[]{:S(2)}) copy-start(bf16[256,2688]{1,0:T(8,128)(2,1)} %all-gather.5.cloned.1.call-done) | copy-start | bytes 4128772
  115.0 8.7 %collective-permute-start.10 = (bf16[256,256]{0,1:T(8,128)(2,1)S(1)}, bf16[256,256]{0,1:T(8,128)(2,1)S(1)}, u32[]{:S(2)}, u32[]{:S(2)}) collective-permute-start(bf16[256,256]{0,1:T(8,128)(2,1)S(1)} %get-tuple-element.17), channel_id=1, source_target_pairs={{6,0},{8,2},{10,4},{12,6},{14,8},{7,1},{9,3},{11,5},{13,7},{15,9},... | collective-permute-start | bytes 393224 | tf_op jit(solution)/shard_map/ppermute | solution.py:17
  116.4 17.4 %collective-permute-start.11 = (bf16[256,256]{0,1:T(8,128)(2,1)S(1)}, bf16[256,256]{0,1:T(8,128)(2,1)S(1)}, u32[]{:S(2)}, u32[]{:S(2)}) collective-permute-start(bf16[256,256]{0,1:T(8,128)(2,1)S(1)} %get-tuple-element.16), channel_id=1, source_target_pairs={{8,0},{10,2},{12,4},{14,6},{9,1},{11,3},{13,5},{15,7},{24,16},{26,... | collective-permute-start | bytes 393224 | tf_op jit(solution)/shard_map/ppermute | solution.py:17
  117.7 16.1 %collective-permute-start.8 = (bf16[256,256]{0,1:T(8,128)(2,1)S(1)}, bf16[256,256]{0,1:T(8,128)(2,1)S(1)}, u32[]{:S(2)}, u32[]{:S(2)}) collective-permute-start(bf16[256,256]{0,1:T(8,128)(2,1)S(1)} %get-tuple-element.15), channel_id=1, source_target_pairs={{2,0},{4,2},{6,4},{8,6},{10,8},{12,10},{14,12},{3,1},{5,3},{7,5},{... | collective-permute-start | bytes 393224 | tf_op jit(solution)/shard_map/ppermute | solution.py:17
  119.0 14.9 %copy-start.15 = (f32[256,128]{0,1:T(8,128)S(1)}, f32[256,128]{0,1:T(8,128)}, u32[]{:S(2)}) copy-start(f32[256,128]{0,1:T(8,128)} %copy-done.14) | copy-start | bytes 393220
  119.0 14.9 %copy-start.41 = (f32[128]{0:T(128)S(1)}, f32[128]{0:T(128)}, u32[]{:S(2)}) copy-start(f32[128]{0:T(128)} %param.24) | copy-start | bytes 1540
  119.0 14.8 %collective-permute-start.9 = (bf16[256,256]{0,1:T(8,128)(2,1)S(1)}, bf16[256,256]{0,1:T(8,128)(2,1)S(1)}, u32[]{:S(2)}, u32[]{:S(2)}) collective-permute-start(bf16[256,256]{0,1:T(8,128)(2,1)S(1)} %get-tuple-element.18), channel_id=1, source_target_pairs={{4,0},{6,2},{8,4},{10,6},{12,8},{14,10},{5,1},{7,3},{9,5},{11,7},{... | collective-permute-start | bytes 393224 | tf_op jit(solution)/shard_map/ppermute | solution.py:17
  121.7 13.2 %copy-start.31 = (bf16[16,128]{1,0:T(8,128)(2,1)S(1)}, bf16[16,128]{1,0:T(8,128)(2,1)}, u32[]{:S(2)}) copy-start(bf16[16,128]{1,0:T(8,128)(2,1)} %param.33) | copy-start | bytes 12292
  121.7 13.4 %copy-start.33 = (bf16[16,128]{1,0:T(8,128)(2,1)S(1)}, bf16[16,128]{1,0:T(8,128)(2,1)}, u32[]{:S(2)}) copy-start(bf16[16,128]{1,0:T(8,128)(2,1)} %param.32) | copy-start | bytes 12292
  139.0 86.7 %all-reduce.6.cloned.1.call-start = ((), (), s32[]{:S(2)}) async-start(), calls=%async_computation.11 | async-start | bytes 139264 | tf_op jit(solution)/shard_map/psum | solution.py:236
  139.8 4.0 %copy-start.19 = (bf16[2688,48]{0,1:T(8,128)(2,1)S(1)}, bf16[2688,48]{0,1:T(8,128)(2,1)}, u32[]{:S(2)}) copy-start(bf16[2688,48]{0,1:T(8,128)(2,1)} %param.30) | copy-start | bytes 774148
  139.8 4.0 %copy-start.24 = (bf16[256,16]{0,1:T(8,128)(2,1)S(1)}, bf16[256,16]{0,1:T(8,128)(2,1)}, u32[]{:S(2)}) copy-start(bf16[256,16]{0,1:T(8,128)(2,1)} %copy-done.23) | copy-start | bytes 24580
  143.7 7.7 %copy-start.5 = (f32[256,256]{0,1:T(8,128)S(1)}, f32[256,256]{0,1:T(8,128)}, u32[]{:S(2)}) copy-start(f32[256,256]{0,1:T(8,128)} %copy-done.4) | copy-start | bytes 786436
  143.7 7.7 %copy-start.12 = (bf16[2688,128]{1,0:T(8,128)(2,1)S(1)}, bf16[2688,128]{1,0:T(8,128)(2,1)}, u32[]{:S(2)}) copy-start(bf16[2688,128]{1,0:T(8,128)(2,1)} %param.28) | copy-start | bytes 2064388
  143.7 156.0 %all-reduce.4.cloned.1.call-start = ((), (), s32[]{:S(2)}) async-start(), calls=%async_computation.8 | async-start | bytes 270336 | tf_op jit(solution)/shard_map/psum | solution.py:235
  151.3 158.8 %reduce-scatter.11.cloned.1.call-start = ((), (), s32[]{:S(2)}) async-start(), calls=%async_computation.7 | async-start | bytes 2064384 | tf_op jit(solution)/shard_map/reduce_scatter | solution.py:224
  155.6 154.5 %copy-start.2 = (bf16[128,2688]{1,0:T(8,128)(2,1)S(1)}, bf16[128,2688]{1,0:T(8,128)(2,1)}, u32[]{:S(2)}) copy-start(bf16[128,2688]{1,0:T(8,128)(2,1)} %param.18) | copy-start | bytes 2064388
  155.6 154.5 %copy-start.22 = (f32[2688]{0:T(1024)S(1)}, f32[2688]{0:T(1024)}, u32[]{:S(2)}) copy-start(f32[2688]{0:T(1024)} %param.22) | copy-start | bytes 32260
  155.6 154.5 %copy-start.39 = (f32[128]{0:T(128)S(1)}, f32[128]{0:T(128)}, u32[]{:S(2)}) copy-start(f32[128]{0:T(128)} %copy-done.38) | copy-start | bytes 1540
  (17 other events, 28.4 us)
Sparse Core Ops, SparseCore 0:
  11.5 12.2 all-gather.2
  54.6 11.7 reduce-scatter.12
  68.6 9.9 reduce-scatter.8
  82.3 10.7 all-gather.4
  139.1 10.3 reduce-scatter.14
  154.5 71.0 all-reduce.5
  230.0 69.7 all-reduce.3
  302.0 8.0 reduce-scatter.10
where the time goes:
time: 321 us; the launch traced here: 320 us
  waiting for transfers between devices  188 us (59%)
  matrix products  51.8 us (16%)
  starting transfers between devices  30.5 us (10%)
  other arithmetic  20.1 us (6%)
  between operations  15.6 us (5%)
  local copies, waits for them, and re-layouts  9.76 us (3%)
  blocking collectives  3.64 us (1%)
    psum x1, waiting for transfers between devices, on_device(): lax.psum(query_up_contribution.astype(jnp.bfloat16), 'ctx')  70 us
    psum x1, waiting for transfers between devices, on_device(): lax.psum(down_term, 'ctx').astype(jnp.float32)  67.5 us
    ppermute x12, starting transfers between devices, passed_along(): lax.ppermute(value, axis, [(source, source + steps) for source in range(l...  30.2 us
    dot_general x10, matrix products, multiply_by_transpose(): lax.dot_general(first_op, second_op, (((1,), (1,)), ((), ())), preferred_...  16.7 us
    ppermute x12, waiting for transfers between devices, passed_along(): lax.ppermute(value, axis, [(source, source + steps) for source in range(l...  13.4 us
    unnamed x10, waiting for transfers between devices  12.5 us
    reduce_scatter x1, waiting for transfers between devices, on_device(): lax.psum_scatter(part_out.astype(jnp.bfloat16), 'tp', scatter_dimension=0...  12.3 us
    unnamed x102, local copies, waits for them, and re-layouts  9.72 us
  transfers between devices with their start and end apart: 20, of which 10 were waited for; matrix products, arithmetic and copies ran while one was open for 10% of the time, Pallas kernels for 0%

commit v1 on v0

v1 whole, which is shorter than its diff:
```python
import jax
import jax.numpy as jnp
from jax import lax
from jax.experimental import pallas as pl
from jax.experimental.pallas import tpu as pltpu
from jax.sharding import PartitionSpec as P

WINDOW = 1024
LANES = 128
NORM_ROWS = 16

epsilon = 1e-06
adapter_scale = 2.0
score_scale = 168.0 ** (-0.5)

bf16 = jnp.bfloat16
f32 = jnp.float32


def norm_rows(source, gain_vec):
    inverse = lax.rsqrt(jnp.mean(source * source, axis=-1, keepdims=True) + epsilon)
    return source * inverse * gain_vec


def norm_back(source, gain_vec, incoming):
    inverse = lax.rsqrt(jnp.mean(source * source, axis=-1, keepdims=True) + epsilon)
    scaled = source * inverse
    upward = incoming * gain_vec
    return inverse * (upward - scaled * jnp.mean(upward * scaled, axis=-1, keepdims=True))


def matrix_product(first_op, second_op):
    return jnp.dot(first_op, second_op, preferred_element_type=f32)


def multiply_by_transpose(first_op, second_op):
    return lax.dot_general(
        first_op, second_op, (((1,), (1,)), ((), ())), preferred_element_type=f32
    )


def window_of(model_width, tp_size):
    slice_width = model_width // tp_size
    if slice_width % LANES == 0:
        return slice_width, slice_width
    width = min(-(-(slice_width + LANES - 1) // LANES) * LANES, model_width)
    if tp_size == 2:
        width = -(-slice_width // LANES) * LANES
    return slice_width, width


def window_start(tp_index, slice_width, width, model_width):
    return jnp.minimum(tp_index * slice_width // LANES * LANES, model_width - width)


def layer_kernel(
    shapes,
    tokens,
    output_gradient,
    documents,
    token_count,
    input_gain,
    query_gain,
    key_gain,
    output_gain,
    query_w,
    key_w,
    value_w,
    output_w,
    down_w,
    query_up,
    key_up,
    value_up,
    out_down,
    out_up,
    layer_out,
    grad_in,
    sums_out,
    normed,
    codes,
    pairs,
    weights,
    attended,
    out_send,
    out_recv,
    mid_send,
    mid_recv,
    pre_norm,
    grad_full,
    small_full,
    pair_grads,
    pair_recv,
    query_pre,
    key_pre,
    pre_grads,
    mid_pad,
    mid_grads,
    mid_grads_recv,
    normed_send,
    normed_recv,
    grad_normed,
    sums_send,
    sums_recv,
    sums_all,
    gather_sems,
    code_sems,
    pair_sems,
    out_sems,
    mid_sems,
    grad_sems,
    small_sems,
    back_sems,
    mid_grad_sems,
    normed_sems,
    sum_sems,
    total_sems,
):
    ctx_size, tp_size, reach, hops = shapes
    rows, model = tokens.shape
    block = documents.shape[1]
    head = key_w.shape[1]
    heads = query_w.shape[1] // head
    rank = key_up.shape[0]
    ctx = lax.axis_index("ctx")
    tp = lax.axis_index("tp")

    def tp_at(step):
        return lax.rem(tp + step, tp_size)

    def ctx_at(step):
        return lax.rem(ctx + step, ctx_size)

    def remote(source, target, sems, slot, where):
        return pltpu.make_async_remote_copy(
            src_ref=source,
            dst_ref=target,
            send_sem=sems.at[0, slot],
            recv_sem=sems.at[1, slot],
            device_id=where,
            device_id_type=pl.DeviceIdType.MESH,
        )

    def rows_of(index):
        return pl.ds(pl.multiple_of(index * rows, rows), rows)

    mine = rows_of(tp)

    barrier = pltpu.get_barrier_semaphore()
    for step in range(1, tp_size):
        pl.semaphore_signal(
            barrier, inc=1, device_id={"tp": tp_at(step)}, device_id_type=pl.DeviceIdType.MESH
        )
    for step in range(1, ctx_size):
        pl.semaphore_signal(
            barrier, inc=1, device_id={"ctx": ctx_at(step)}, device_id_type=pl.DeviceIdType.MESH
        )

    def norm_chunk(index, carry):
        at = pl.ds(pl.multiple_of(index * NORM_ROWS, NORM_ROWS), NORM_ROWS)
        to = pl.ds(pl.multiple_of(tp * rows + index * NORM_ROWS, NORM_ROWS), NORM_ROWS)
        normed[to, :] = norm_rows(tokens[at, :].astype(f32), input_gain[...]).astype(bf16)
        return carry

    lax.fori_loop(0, rows // NORM_ROWS, norm_chunk, 0)

    lane_pos = lax.broadcasted_iota(jnp.int32, (1, block), 1)
    valid_lane = (lane_pos < token_count[0]).astype(f32)
    valid_sub = (
        lax.broadcasted_iota(jnp.int32, (block, 1), 0) < token_count[0]
    ).astype(f32)
    own_codes = jnp.where(lane_pos < token_count[0], documents[...] + 1, 0)
    codes[0] = jnp.broadcast_to(own_codes, codes.shape[1:])
    for hop in range(1, hops + 1):

        @pl.when(ctx < hop)
        def _(hop=hop):
            codes[hop] = jnp.zeros(codes.shape[1:], codes.dtype)
            pairs[hop] = jnp.zeros(pairs.shape[1:], pairs.dtype)

        @pl.when(ctx + hop >= ctx_size)
        def _(hop=hop):
            pair_recv[hop - 1] = jnp.zeros(pair_recv.shape[1:], pair_recv.dtype)

    pl.semaphore_wait(barrier, tp_size - 1 + ctx_size - 1)

    gathers = []
    for step in range(1, tp_size):
        copy = remote(
            normed.at[mine], normed.at[mine], gather_sems, step - 1, {"tp": tp_at(step)}
        )
        copy.start()
        gathers.append(copy)

    def code_copy(hop):
        return remote(codes.at[0], codes.at[hop], code_sems, hop - 1, {"ctx": ctx_at(hop)})

    def pair_copy(hop):
        return remote(pairs.at[0], pairs.at[hop], pair_sems, hop - 1, {"ctx": ctx_at(hop)})

    def back_copy(hop):
        return remote(
            pair_grads.at[hop - 1],
            pair_recv.at[hop - 1],
            back_sems,
            hop - 1,
            {"ctx": ctx_at(ctx_size - hop)},
        )

    for hop in range(1, hops + 1):

        @pl.when(ctx + hop < ctx_size)
        def _(hop=hop):
            code_copy(hop).start()

    for copy in gathers:
        copy.wait()

    inputs = normed[...]
    middles = matrix_product(inputs, down_w[...]).astype(bf16)
    mid_pad[...] = jnp.zeros(mid_pad.shape, f32)
    mid_pad[:, : 3 * rank] = middles.astype(f32)

    def projected(weight, up, place):
        return matrix_product(inputs, weight[...]) + adapter_scale * matrix_product(
            middles[:, place * rank : (place + 1) * rank], up[...]
        )

    key_pre[...] = projected(key_w, key_up, 1)
    pairs[0, :, :head] = norm_rows(key_pre[...], key_gain[...]).astype(bf16)
    pairs[0, :, head:] = projected(value_w, value_up, 2).astype(bf16)
    for hop in range(1, hops + 1):

        @pl.when(ctx + hop < ctx_size)
        def _(hop=hop):
            pair_copy(hop).start()

    query_pre[...] = projected(query_w, query_up, 0)
    query_list = [
        norm_rows(query_pre[:, h * head : (h + 1) * head], query_gain[...]) for h in range(heads)
    ]
    query_rows = jnp.concatenate(query_list, axis=0).astype(bf16)
    query_cols = jnp.concatenate([q.T for q in query_list], axis=1).astype(bf16)

    sub = lax.broadcasted_iota(jnp.int32, (block, block), 0)
    lane = lax.broadcasted_iota(jnp.int32, (block, block), 1)
    wanted = (documents[...] + 1).astype(f32)
    totals = jnp.zeros((1, heads * block), f32)
    outputs = jnp.zeros((head, heads * block), f32)
    for hop in range(hops + 1):
        if hop > 0:

            @pl.when(ctx >= hop)
            def _(hop=hop):
                code_copy(hop).wait_recv()
                pair_copy(hop).wait_recv()

        code_row = codes[hop][0:1, :].astype(f32)
        code_col = jnp.sum(jnp.where(sub == lane, code_row, 0.0), axis=1, keepdims=True)
        allowed = code_col == wanted
        if hop == 0:
            allowed = (sub == lane) | ((sub < lane) & allowed)
        if hop == reach:
            allowed = (sub > lane) & allowed
        allowed = allowed.astype(f32)
        allowed = jnp.concatenate([allowed] * heads, axis=1)
        scores = matrix_product(pairs[hop, :, :head], query_cols) * score_scale
        exps = jnp.where(allowed > 0.0, jnp.exp(scores), 0.0)
        totals = totals + jnp.sum(exps, axis=0, keepdims=True)
        exps = exps.astype(bf16)
        weights[hop] = exps
        values_cols = pairs[hop, :, head:].astype(f32).T.astype(bf16)
        outputs = outputs + matrix_product(values_cols, exps)
    inverse_totals = 1.0 / totals
    outputs = outputs * inverse_totals
    for h in range(heads):
        piece = outputs[:, h * block : (h + 1) * block] * valid_lane
        attended[:, h * head : (h + 1) * head] = piece.T.astype(bf16)

    mid_send[...] = jnp.zeros(mid_send.shape, bf16)
    out_copies = []
    for step in range(1, tp_size):
        theirs = attended[rows_of(tp_at(step)), :]
        mid_send[step - 1, :, :rank] = matrix_product(theirs, out_down[...]).astype(bf16)
        out_send[step - 1] = matrix_product(theirs, output_w[...]).astype(bf16)
        for source, target, sems in (
            (mid_send, mid_recv, mid_sems),
            (out_send, out_recv, out_sems),
        ):
            copy = remote(
                source.at[step - 1], target.at[step - 1], sems, step - 1, {"tp": tp_at(step)}
            )
            copy.start()
            out_copies.append(copy)
    own_rows = attended[mine, :]
    mid_sum = matrix_product(own_rows, out_down[...]).astype(bf16).astype(f32)
    pre_norm[...] = matrix_product(own_rows, output_w[...])
    for copy in out_copies:
        copy.wait()
    for step in range(1, tp_size):
        mid_sum = mid_sum + mid_recv[step - 1, :, :rank].astype(f32)
    mid_out = mid_sum.astype(bf16)
    pre_norm[...] += adapter_scale * matrix_product(mid_out, out_up[...])

    def out_chunk(index, carry):
        at = pl.ds(pl.multiple_of(index * NORM_ROWS, NORM_ROWS), NORM_ROWS)
        to = pl.ds(pl.multiple_of(tp * rows + index * NORM_ROWS, NORM_ROWS), NORM_ROWS)
        held = pre_norm[at, :]
        for step in range(1, tp_size):
            held = held + out_recv[step - 1, at, :].astype(f32)
        layer_out[at, :] = norm_rows(held, output_gain[...]).astype(bf16)
        grad_full[to, :] = norm_back(
            held, output_gain[...], output_gradient[at, :].astype(f32)
        ).astype(bf16)
        return carry

    lax.fori_loop(0, rows // NORM_ROWS, out_chunk, 0)

    grad_copies = []
    for step in range(1, tp_size):
        copy = remote(
            grad_full.at[mine], grad_full.at[mine], grad_sems, step - 1, {"tp": tp_at(step)}
        )
        copy.start()
        grad_copies.append(copy)
    grad_mid_out = adapter_scale * multiply_by_transpose(grad_full[mine, :], out_up[...])
    small_full[mine, :] = jnp.zeros((rows, 2 * LANES), bf16)
    small_full[mine, :rank] = grad_mid_out.astype(bf16)
    small_full[mine, LANES : LANES + rank] = mid_out
    for step in range(1, tp_size):
        copy = remote(
            small_full.at[mine], small_full.at[mine], small_sems, step - 1, {"tp": tp_at(step)}
        )
        copy.start()
        grad_copies.append(copy)
    for copy in grad_copies:
        copy.wait()

    grad_att = (
        multiply_by_transpose(grad_full[...], output_w[...])
        + multiply_by_transpose(small_full[:, :rank], out_down[...])
    ) * valid_sub
    grad_cols = jnp.concatenate(
        [grad_att[:, h * head : (h + 1) * head].T for h in range(heads)], axis=1
    ).astype(bf16)
    grad_float = grad_cols.astype(f32)
    inner = jnp.sum(grad_float * outputs, axis=0, keepdims=True)
    grad_rows = (grad_float * inverse_totals).T.astype(bf16)
    row_scale = inverse_totals * score_scale

    query_back = jnp.zeros((head, heads * block), f32)
    own_keys = own_values = None
    for hop in range(hops, -1, -1):
        keys = pairs[hop, :, :head]
        exps = weights[hop]
        probs_back = matrix_product(pairs[hop, :, head:], grad_cols)
        scores_back = (exps.astype(f32) * ((probs_back - inner) * row_scale)).astype(bf16)
        keys_back = matrix_product(scores_back, query_rows)
        values_back = matrix_product(exps, grad_rows)
        query_back = query_back + matrix_product(keys.astype(f32).T.astype(bf16), scores_back)
        if hop > 0:
            pair_grads[hop - 1, :, :head] = keys_back.astype(bf16)
            pair_grads[hop - 1, :, head:] = values_back.astype(bf16)

            @pl.when(ctx >= hop)
            def _(hop=hop):
                back_copy(hop).start()

        else:
            own_keys, own_values = keys_back, values_back
    query_width = heads * head
    for h in range(heads):
        at = slice(h * head, (h + 1) * head)
        pre_grads[:, at] = norm_back(
            query_pre[:, at], query_gain[...], query_back[:, h * block : (h + 1) * block].T
        ).astype(bf16)
    for hop in range(1, hops + 1):

        @pl.when(ctx + hop < ctx_size)
        def _(hop=hop):
            back_copy(hop).wait_recv()

        own_keys = own_keys + pair_recv[hop - 1, :, :head].astype(f32)
        own_values = own_values + pair_recv[hop - 1, :, head:].astype(f32)
    key_at = slice(query_width, query_width + head)
    value_at = slice(query_width + head, query_width + 2 * head)
    pre_grads[:, key_at] = norm_back(key_pre[...], key_gain[...], own_keys).astype(bf16)
    pre_grads[:, value_at] = own_values.astype(bf16)

    mid_grads[...] = jnp.zeros(mid_grads.shape, bf16)
    for place, (at, up) in enumerate(
        ((slice(0, query_width), query_up), (key_at, key_up), (value_at, value_up))
    ):
        mid_grads[:, place * rank : (place + 1) * rank] = (
            adapter_scale * multiply_by_transpose(pre_grads[:, at], up[...])
        ).astype(bf16)
    last_copies = []
    for step in range(1, tp_size):
        copy = remote(
            mid_grads, mid_grads_recv.at[step - 1], mid_grad_sems, step - 1, {"tp": tp_at(step)}
        )
        copy.start()
        last_copies.append(copy)

    def input_part(which):
        grads = pre_grads[which, :]
        return (
            multiply_by_transpose(grads[:, :query_width], query_w[...])
            + multiply_by_transpose(grads[:, key_at], key_w[...])
            + multiply_by_transpose(grads[:, value_at], value_w[...])
            + multiply_by_transpose(mid_grads[which, : 3 * rank], down_w[...])
        )

    normed_copies = []
    for step in range(1, tp_size):
        normed_send[step - 1] = input_part(rows_of(tp_at(step))).astype(bf16)
        copy = remote(
            normed_send.at[step - 1],
            normed_recv.at[step - 1],
            normed_sems,
            step - 1,
            {"tp": tp_at(step)},
        )
        copy.start()
        normed_copies.append(copy)

    slice_width, width = window_of(model, tp_size)
    start = window_start(tp, slice_width, width, model)
    window = pl.ds(pl.multiple_of(start, LANES), width)
    for copy in last_copies:
        copy.wait()
    mid_total = mid_grads[...].astype(f32)
    for step in range(1, tp_size):
        mid_total = mid_total + mid_grads_recv[step - 1].astype(f32)
    mid_total = mid_total.T[: 3 * rank].astype(bf16)
    middle_cols = mid_pad[...].T[: 3 * rank].astype(bf16)
    small_cols = small_full[...].astype(f32).T
    grad_mid_cols = small_cols[:rank].astype(bf16)
    mid_out_cols = small_cols[LANES : LANES + rank].astype(bf16)
    main_terms = jnp.concatenate(
        [
            matrix_product(mid_total, normed[:, window]),
            adapter_scale * matrix_product(mid_out_cols, grad_full[:, window]),
        ],
        axis=0,
    ).astype(bf16)
    up_terms = [
        adapter_scale * matrix_product(middle_cols[:rank], pre_grads[:, :query_width]),
        adapter_scale
        * jnp.concatenate(
            [
                matrix_product(middle_cols[rank : 2 * rank], pre_grads[:, key_at]),
                matrix_product(middle_cols[2 * rank :], pre_grads[:, value_at]),
            ],
            axis=1,
        ),
        matrix_product(grad_mid_cols, attended[...]),
        jnp.zeros((rank, query_width), f32),
    ]
    piece_width = sums_send.shape[2]
    padding = piece_width * ctx_size - width - query_width
    pieces = [main_terms, jnp.concatenate(up_terms, axis=0).astype(bf16)]
    if padding > 0:
        pieces.append(jnp.zeros((4 * rank, padding), bf16))
    every_term = jnp.concatenate(pieces, axis=1)
    for index in range(ctx_size):
        sums_send[index] = every_term[:, index * piece_width : (index + 1) * piece_width]
    sum_copies = []
    for step in range(1, ctx_size):
        copy = remote(
            sums_send.at[ctx_at(step)],
            sums_recv.at[step - 1],
            sum_sems,
            step - 1,
            {"ctx": ctx_at(step)},
        )
        copy.start()
        sum_copies.append(copy)

    grad_normed[...] = input_part(mine)
    for copy in sum_copies:
        copy.wait()
    total = sums_send[ctx].astype(f32)
    for step in range(1, ctx_size):
        total = total + sums_recv[step - 1].astype(f32)
    sums_all[ctx] = total.astype(bf16)
    total_copies = []
    for step in range(1, ctx_size):
        copy = remote(
            sums_all.at[ctx], sums_all.at[ctx], total_sems, step - 1, {"ctx": ctx_at(step)}
        )
        copy.start()
        total_copies.append(copy)

    for copy in normed_copies:
        copy.wait()

    def in_chunk(index, carry):
        at = pl.ds(pl.multiple_of(index * NORM_ROWS, NORM_ROWS), NORM_ROWS)
        incoming = grad_normed[at, :]
        for step in range(1, tp_size):
            incoming = incoming + normed_recv[step - 1, at, :].astype(f32)
        grad_in[at, :] = norm_back(
            tokens[at, :].astype(f32), input_gain[...], incoming
        ).astype(bf16)
        return carry

    lax.fori_loop(0, rows // NORM_ROWS, in_chunk, 0)

    for copy in total_copies:
        copy.wait()
    for index in range(ctx_size):
        sums_out[:, index * piece_width : (index + 1) * piece_width] = sums_all[index].astype(f32)

    for hop in range(1, hops + 1):

        @pl.when(ctx + hop < ctx_size)
        def _(hop=hop):
            code_copy(hop).wait_send()
            pair_copy(hop).wait_send()

        @pl.when(ctx >= hop)
        def _(hop=hop):
            back_copy(hop).wait_send()


def on_device(
    tokens,
    output_gradient,
    document_index,
    real_token_count,
    input_norm_gain,
    query_norm_gain,
    key_norm_gain,
    output_norm_gain,
    query_projection,
    key_projection,
    value_projection,
    output_projection,
    adapter_down_maps,
    adapter_query_up,
    adapter_key_up,
    adapter_value_up,
    adapter_output_down,
    adapter_output_up,
):
    rows, model = tokens.shape
    block = document_index.shape[0]
    head = key_projection.shape[1]
    query_width = query_projection.shape[1]
    rank = adapter_key_up.shape[0]
    ctx_size = lax.axis_size("ctx")
    tp_size = lax.axis_size("tp")
    tp_index = lax.axis_index("tp")
    reach = WINDOW // block
    hops = min(reach, ctx_size - 1)
    peers = max(tp_size - 1, 1)
    slice_width, width = window_of(model, tp_size)
    piece_width = -(-(width + query_width) // (LANES * ctx_size)) * LANES

    def kernel(*refs):
        layer_kernel((ctx_size, tp_size, reach, hops), *refs)

    whole = pl.BlockSpec(memory_space=pltpu.VMEM)
    in_specs = [whole] * 18
    in_specs[3] = pl.BlockSpec(memory_space=pltpu.SMEM)
    layer_out, grad_in, sums = pl.pallas_call(
        kernel,
        out_shape=(
            jax.ShapeDtypeStruct((rows, model), bf16),
            jax.ShapeDtypeStruct((rows, model), bf16),
            jax.ShapeDtypeStruct((4 * rank, piece_width * ctx_size), f32),
        ),
        in_specs=in_specs,
        out_specs=(whole, whole, whole),
        scratch_shapes=[
            pltpu.VMEM((block, model), bf16),
            pltpu.VMEM((hops + 1, 8, block), jnp.int32),
            pltpu.VMEM((hops + 1, block, 2 * head), bf16),
            pltpu.VMEM((hops + 1, block, query_width // head * block), bf16),
            pltpu.VMEM((block, query_width), bf16),
            pltpu.VMEM((peers, rows, model), bf16),
            pltpu.VMEM((peers, rows, model), bf16),
            pltpu.VMEM((peers, rows, LANES), bf16),
            pltpu.VMEM((peers, rows, LANES), bf16),
            pltpu.VMEM((rows, model), f32),
            pltpu.VMEM((block, model), bf16),
            pltpu.VMEM((block, 2 * LANES), bf16),
            pltpu.VMEM((hops, block, 2 * head), bf16),
            pltpu.VMEM((hops, block, 2 * head), bf16),
            pltpu.VMEM((block, query_width), f32),
            pltpu.VMEM((block, head), f32),
            pltpu.VMEM((block, query_width + 2 * head), bf16),
            pltpu.VMEM((block, LANES), f32),
            pltpu.VMEM((block, LANES), bf16),
            pltpu.VMEM((peers, block, LANES), bf16),
            pltpu.VMEM((peers, rows, model), bf16),
            pltpu.VMEM((peers, rows, model), bf16),
            pltpu.VMEM((rows, model), f32),
            pltpu.VMEM((ctx_size, 4 * rank, piece_width), bf16),
            pltpu.VMEM((ctx_size - 1, 4 * rank, piece_width), bf16),
            pltpu.VMEM((ctx_size, 4 * rank, piece_width), bf16),
            pltpu.SemaphoreType.DMA((2, peers)),
            pltpu.SemaphoreType.DMA((2, hops)),
            pltpu.SemaphoreType.DMA((2, hops)),
            pltpu.SemaphoreType.DMA((2, peers)),
            pltpu.SemaphoreType.DMA((2, peers)),
            pltpu.SemaphoreType.DMA((2, peers)),
            pltpu.SemaphoreType.DMA((2, peers)),
            pltpu.SemaphoreType.DMA((2, hops)),
            pltpu.SemaphoreType.DMA((2, peers)),
            pltpu.SemaphoreType.DMA((2, peers)),
            pltpu.SemaphoreType.DMA((2, ctx_size - 1)),
            pltpu.SemaphoreType.DMA((2, ctx_size - 1)),
        ],
        compiler_params=pltpu.CompilerParams(
            collective_id=0, has_side_effects=True, vmem_limit_bytes=56 * 1024 * 1024
        ),
    )(
        tokens,
        output_gradient,
        document_index.reshape(1, block),
        real_token_count,
        input_norm_gain.reshape(1, model),
        query_norm_gain.reshape(1, head),
        key_norm_gain.reshape(1, head),
        output_norm_gain.reshape(1, model),
        query_projection,
        key_projection,
        value_projection,
        output_projection,
        adapter_down_maps,
        adapter_query_up,
        adapter_key_up,
        adapter_value_up,
        adapter_output_down,
        adapter_output_up,
    )
    offset = tp_index * slice_width - window_start(tp_index, slice_width, width, model)
    share = lax.dynamic_slice_in_dim(sums[:, :width], offset, slice_width, 1)
    ups = sums[:, width : width + query_width]
    return (
        layer_out,
        grad_in,
        share[: 3 * rank].T,
        ups[:rank],
        ups[rank : 2 * rank, :head],
        ups[rank : 2 * rank, head : 2 * head],
        ups[2 * rank : 3 * rank].T,
        share[3 * rank :],
    )


def solution(mesh):
    in_specs = (
        P(("groups", "ctx", "tp"), None),
        P(("groups", "ctx", "tp"), None),
        P(("groups", "ctx")),
        P(("groups", "ctx")),
        P(),
        P(),
        P(),
        P(),
        P(None, "tp"),
        P(None, "tp"),
        P(None, "tp"),
        P("tp", None),
        P(),
        P(None, "tp"),
        P(None, "tp"),
        P(None, "tp"),
        P("tp", None),
        P(),
    )
    out_specs = (
        P(("groups", "ctx", "tp"), None),
        P(("groups", "ctx", "tp"), None),
        P(("groups", "tp"), None),
        P("groups", "tp"),
        P("groups", "tp"),
        P("groups", "tp"),
        P(("groups", "tp"), None),
        P("groups", "tp"),
    )
    return jax.shard_map(
        on_device, mesh=mesh, in_specs=in_specs, out_specs=out_specs, check_vma=False
    )
```

time: 321 us -> 83.4 us (0.26)
  waiting for transfers between devices: 188 us -> 0 us
  Pallas kernels: 0 us -> 68.5 us
  matrix products: 51.8 us -> 0 us
  starting transfers between devices: 30.5 us -> 0 us
  other arithmetic: 20.1 us -> 0 us
  between operations: 15.6 us -> 1.33 us
  blocking collectives: 3.64 us -> 0 us
  local copies, waits for them, and re-layouts: 9.76 us -> 13.2 us
    psum x2 -> x0, waiting for transfers between devices: 138 us -> none  [the longest x1 70 us: on_device(): lax.psum(query_up_contribution.astype(jnp.bfloat16), 'ctx')]
    pallas_call x0 -> x1, Pallas kernels: none -> 68.5 us  [on_device(): pl.pallas_call(kernel, out_shape=(jax.ShapeDtypeStruct((rows, model), bf1...]
    dot_general x31 -> x0, matrix products: 48.4 us -> none  [the longest x10 16.7 us: multiply_by_transpose(): lax.dot_general(first_op, second_op, (((1,), (1,)), ((), ())), preferred_...]
    ppermute x12 -> x0, starting transfers between devices: 30.2 us -> none  [passed_along(): lax.ppermute(value, axis, [(source, source + steps) for source in range(l...]
    reduce_scatter x2 -> x0, waiting for transfers between devices: 21 us -> none  [the longest x1 12.3 us: on_device(): lax.psum_scatter(part_out.astype(jnp.bfloat16), 'tp', scatter_dimension=0...]
    convert_element_type x13 -> x0, other arithmetic: 14.4 us -> none  [the longest x1 2.17 us: on_device(): normed_rows = norm_rows(tok_float, input_norm_gain).astype(jnp.bfloat16)]
    ppermute x12 -> x0, waiting for transfers between devices: 13.4 us -> none  [passed_along(): lax.ppermute(value, axis, [(source, source + steps) for source in range(l...]
    unnamed x10 -> x0, waiting for transfers between devices: 12.5 us -> none
  transfers between devices with their start and end apart: 20 -> 0, of which waited for: 10 -> 0; matrix products, arithmetic and copies ran while one was open for 10% -> 0% of each run, Pallas kernels for 0% -> 0%
where the time goes in v1:
time: 83.4 us; the launch traced here: 83 us
  Pallas kernels  68.5 us (82%)
  local copies, waits for them, and re-layouts  13.2 us (16%)
  between operations  1.33 us (2%)
    pallas_call x1, Pallas kernels, on_device(): pl.pallas_call(kernel, out_shape=(jax.ShapeDtypeStruct((rows, model), bf1...  68.5 us
    unnamed x8, local copies, waits for them, and re-layouts  5.2 us

profile of v1, /device:TPU:0, one launch (start us, length us, event | category | flops | bytes accessed | tf_op | source)
XLA Modules:
  0.0 83.0 jit_solution(8334733029036940752)
XLA Ops:
  1.3 1.3 %reshape.32.refs_4_ = f32[1,2688]{1,0:T(1,128)} reshape(f32[2688]{0:T(1024)} %param.22) | data formatting | bytes 21504 | tf_op jit(solution)/shard_map/reshape | solution.py:623
  2.6 1.3 %reshape.35.refs_7_ = f32[1,2688]{1,0:T(1,128)} reshape(f32[2688]{0:T(1024)} %param.25) | data formatting | bytes 21504 | tf_op jit(solution)/shard_map/reshape | solution.py:626
  3.9 2.1 %copy.26.refs_12_ = bf16[2688,48]{1,0:T(8,128)(2,1)} copy(bf16[2688,48]{0,1:T(8,128)(2,1)} %param.30) | data formatting | bytes 516096 | tf_op args[12]
  6.0 1.4 %copy.27.refs_16_ = bf16[256,16]{1,0:T(8,128)(2,1)} copy(bf16[256,16]{0,1:T(8,128)(2,1)} %param.34) | data formatting | bytes 16384 | tf_op args[16]
  7.4 68.5 %shard_map.233 = (bf16[128,2688]{1,0:T(8,128)(2,1)}, bf16[128,2688]{1,0:T(8,128)(2,1)}, f32[64,2048]{1,0:T(8,128)}) custom-call(bf16[128,2688]{1,0:T(8,128)(2,1)} %refs_0_.1, bf16[128,2688]{1,0:T(8,128)(2,1)} %refs_1_.1, s32[1,256]{1,0:T(1,128)} %bitcast.7, s32[1]{0:T(128)S(6)} %copy.30.refs_3_, f32[1,2688]{1,0:T(1,128)} %reshape.32.refs_4_, ...), custom_call_target="tpu_custom_call" | custom-call | tf_op jit(solution)/shard_map/pallas_call | solution.py:566
  75.9 0.0 copy-start.1
  75.9 0.0 copy-start
  75.9 1.1 %slice.26 = f32[64,1408]{1,0:T(8,128)S(1)} slice(f32[64,2048]{1,0:T(8,128)} %get-tuple-element.13), slice={[0:64], [0:1408]} | slice | bytes 720896 | tf_op jit(solution)/shard_map/slice | solution.py:639
  77.1 0.8 %dynamic-slice_bitcast_fusion = f32[1344,48]{0,1:T(8,128)} fusion(f32[64,1408]{1,0:T(8,128)S(1)} %slice.26, s32[]{:T(128)S(6)} %select_n.9), kind=kLoop, calls=%fused_computation | loop fusion | bytes 516100 | tf_op jit(solution)/shard_map/transpose | solution.py:644
  77.9 1.3 %slice_bitcast_fusion = (f32[256,16]{0,1:T(8,128)}, f32[16,256]{1,0:T(8,128)}) fusion(f32[64,2048]{1,0:T(8,128)} %get-tuple-element.13), kind=kLoop, calls=%fused_computation.1 | loop fusion | bytes 65536 | tf_op jit(solution)/shard_map/transpose | solution.py:648
  79.3 1.3 %fusion = (f32[16,128]{1,0:T(8,128)}, f32[16,128]{1,0:T(8,128)}) fusion(f32[64,2048]{1,0:T(8,128)} %get-tuple-element.13), kind=kLoop, calls=%fused_computation.2 | loop fusion | bytes 32768 | tf_op jit(solution)/shard_map/slice | solution.py:647
  80.6 0.7 dynamic-slice.1
  81.3 0.0 copy-done.1
  81.3 0.8 %copy.31 = bf16[128,2688]{1,0:T(8,128)(2,1)} copy(bf16[128,2688]{1,0:T(8,128)(2,1)S(1)} %copy-done.1) | data formatting | bytes 1376256
  82.2 0.0 copy-done
  82.2 0.8 %copy.32 = bf16[128,2688]{1,0:T(8,128)(2,1)} copy(bf16[128,2688]{1,0:T(8,128)(2,1)S(1)} %copy-done) | data formatting | bytes 1376256
Async XLA Ops:
  75.9 5.4 %copy-start.1 = (bf16[128,2688]{1,0:T(8,128)(2,1)S(1)}, bf16[128,2688]{1,0:T(8,128)(2,1)}, u32[]{:S(2)}) copy-start(bf16[128,2688]{1,0:T(8,128)(2,1)} %get-tuple-element.26) | copy-start | bytes 2064388
  75.9 6.2 %copy-start = (bf16[128,2688]{1,0:T(8,128)(2,1)S(1)}, bf16[128,2688]{1,0:T(8,128)(2,1)}, u32[]{:S(2)}) copy-start(bf16[128,2688]{1,0:T(8,128)(2,1)} %get-tuple-element.27) | copy-start | bytes 2064388

commit v2 on v1

--- a/solution.py
+++ b/solution.py
@@ -59,10 +59,10 @@
     output_gradient,
     documents,
     token_count,
-    input_gain,
+    input_gain_vec,
     query_gain,
     key_gain,
-    output_gain,
+    output_gain_vec,
     query_w,
     key_w,
     value_w,
@@ -75,7 +75,14 @@
     out_up,
     layer_out,
     grad_in,
-    sums_out,
+    down_out_rows,
+    query_up_out,
+    key_up_out,
+    value_up_out,
+    out_down_out,
+    out_up_out,
+    input_gain,
+    output_gain,
     normed,
     codes,
     pairs,
@@ -155,6 +162,9 @@
             barrier, inc=1, device_id={"ctx": ctx_at(step)}, device_id_type=pl.DeviceIdType.MESH
         )
 
+    input_gain[...] = input_gain_vec[...].reshape(1, model)
+    output_gain[...] = output_gain_vec[...].reshape(1, model)
+
     def norm_chunk(index, carry):
         at = pl.ds(pl.multiple_of(index * NORM_ROWS, NORM_ROWS), NORM_ROWS)
         to = pl.ds(pl.multiple_of(tp * rows + index * NORM_ROWS, NORM_ROWS), NORM_ROWS)
@@ -177,9 +187,29 @@
             codes[hop] = jnp.zeros(codes.shape[1:], codes.dtype)
             pairs[hop] = jnp.zeros(pairs.shape[1:], pairs.dtype)
 
-        @pl.when(ctx + hop >= ctx_size)
-        def _(hop=hop):
-            pair_recv[hop - 1] = jnp.zeros(pair_recv.shape[1:], pair_recv.dtype)
+    odd = lax.rem(ctx, 2) == 1
+    even = jnp.logical_not(odd)
+    has_up = ctx + 2 < ctx_size
+    partner = {"ctx": ctx + 1 - 2 * lax.rem(ctx, 2)}
+    above = {"ctx": ctx_at(2)}
+    below = {"ctx": ctx_at(ctx_size - 2)}
+    arrives = (
+        (even & (ctx >= 2)) | (odd & (ctx >= 5)),
+        has_up & (ctx >= 2),
+        even | (ctx >= 3),
+        has_up,
+    )
+    sends = (
+        (even & (ctx >= 4)) | (odd & (ctx >= 3)),
+        ctx >= 4,
+        odd | (ctx >= 2),
+        ctx >= 2,
+    )
+    for place in range(4):
+
+        @pl.when(jnp.logical_not(arrives[place]))
+        def _(place=place):
+            pair_recv[place] = jnp.zeros(pair_recv.shape[1:], pair_recv.dtype)
 
     pl.semaphore_wait(barrier, tp_size - 1 + ctx_size - 1)
 
@@ -194,17 +224,14 @@
     def code_copy(hop):
         return remote(codes.at[0], codes.at[hop], code_sems, hop - 1, {"ctx": ctx_at(hop)})
 
-    def pair_copy(hop):
-        return remote(pairs.at[0], pairs.at[hop], pair_sems, hop - 1, {"ctx": ctx_at(hop)})
-
-    def back_copy(hop):
-        return remote(
-            pair_grads.at[hop - 1],
-            pair_recv.at[hop - 1],
-            back_sems,
-            hop - 1,
-            {"ctx": ctx_at(ctx_size - hop)},
-        )
+    def pair_copy(source, target, where):
+        return remote(pairs.at[source], pairs.at[target], pair_sems, target - 1, where)
+
+    def back_copy(hop, place, where):
+        return remote(pair_grads.at[hop - 1], pair_recv.at[place], back_sems, place, where)
+
+    pair_arrives = {1: odd | (ctx >= 2), 2: ctx >= 2, 3: ctx >= 3, 4: ctx >= 4}
+    pair_arrives[3] = (odd & (ctx >= 3)) | (even & (ctx >= 4))
 
     for hop in range(1, hops + 1):
 
@@ -216,7 +243,7 @@
         copy.wait()
 
     inputs = normed[...]
-    middles = matrix_product(inputs, down_w[...]).astype(bf16)
+    middles = multiply_by_transpose(inputs, down_w[...]).astype(bf16)
     mid_pad[...] = jnp.zeros(mid_pad.shape, f32)
     mid_pad[:, : 3 * rank] = middles.astype(f32)
 
@@ -228,11 +255,14 @@
     key_pre[...] = projected(key_w, key_up, 1)
     pairs[0, :, :head] = norm_rows(key_pre[...], key_gain[...]).astype(bf16)
     pairs[0, :, head:] = projected(value_w, value_up, 2).astype(bf16)
-    for hop in range(1, hops + 1):
-
-        @pl.when(ctx + hop < ctx_size)
-        def _(hop=hop):
-            pair_copy(hop).start()
+
+    @pl.when(has_up)
+    def _():
+        pair_copy(0, 2, above).start()
+
+    @pl.when(even)
+    def _():
+        pair_copy(0, 1, partner).start()
 
     query_pre[...] = projected(query_w, query_up, 0)
     query_list = [
@@ -246,14 +276,42 @@
     wanted = (documents[...] + 1).astype(f32)
     totals = jnp.zeros((1, heads * block), f32)
     outputs = jnp.zeros((head, heads * block), f32)
-    for hop in range(hops + 1):
-        if hop > 0:
-
-            @pl.when(ctx >= hop)
-            def _(hop=hop):
-                code_copy(hop).wait_recv()
-                pair_copy(hop).wait_recv()
-
+    for hop in range(1, hops + 1):
+
+        @pl.when(ctx >= hop)
+        def _(hop=hop):
+            code_copy(hop).wait_recv()
+
+    def receive_pair(hop):
+        @pl.when(pair_arrives[hop])
+        def _():
+            pair_copy(0, hop, partner).wait_recv()
+
+    receive_pair(2)
+
+    @pl.when(has_up & (ctx >= 2))
+    def _():
+        pair_copy(2, 4, above).start()
+
+    @pl.when(even & (ctx >= 2))
+    def _():
+        pair_copy(2, 3, partner).start()
+
+    @pl.when(odd & (ctx >= 2))
+    def _():
+        pair_copy(2, 1, partner).start()
+
+    for hop in (0, 2, 1, 4, 3):
+        if hop == 1:
+            receive_pair(1)
+            receive_pair(4)
+
+            @pl.when(odd & (ctx >= 4))
+            def _():
+                pair_copy(4, 3, partner).start()
+
+        if hop == 3:
+            receive_pair(3)
         code_row = codes[hop][0:1, :].astype(f32)
         code_col = jnp.sum(jnp.where(sub == lane, code_row, 0.0), axis=1, keepdims=True)
         allowed = code_col == wanted
@@ -280,7 +338,7 @@
     out_copies = []
     for step in range(1, tp_size):
         theirs = attended[rows_of(tp_at(step)), :]
-        mid_send[step - 1, :, :rank] = matrix_product(theirs, out_down[...]).astype(bf16)
+        mid_send[step - 1, :, :rank] = multiply_by_transpose(theirs, out_down[...]).astype(bf16)
         out_send[step - 1] = matrix_product(theirs, output_w[...]).astype(bf16)
         for source, target, sems in (
             (mid_send, mid_recv, mid_sems),
@@ -292,7 +350,7 @@
             copy.start()
             out_copies.append(copy)
     own_rows = attended[mine, :]
-    mid_sum = matrix_product(own_rows, out_down[...]).astype(bf16).astype(f32)
+    mid_sum = multiply_by_transpose(own_rows, out_down[...]).astype(bf16).astype(f32)
     pre_norm[...] = matrix_product(own_rows, output_w[...])
     for copy in out_copies:
         copy.wait()
@@ -337,7 +395,7 @@
 
     grad_att = (
         multiply_by_transpose(grad_full[...], output_w[...])
-        + multiply_by_transpose(small_full[:, :rank], out_down[...])
+        + matrix_product(small_full[:, :rank], out_down[...])
     ) * valid_sub
     grad_cols = jnp.concatenate(
         [grad_att[:, h * head : (h + 1) * head].T for h in range(heads)], axis=1
@@ -348,8 +406,20 @@
     row_scale = inverse_totals * score_scale
 
     query_back = jnp.zeros((head, heads * block), f32)
-    own_keys = own_values = None
-    for hop in range(hops, -1, -1):
+    odd_share = odd.astype(f32)
+    even_share = 1.0 - odd_share
+
+    def receive_back(place):
+        @pl.when(arrives[place])
+        def _():
+            back_copy(1, place, partner).wait_recv()
+
+    def send_back(hop, place, where, sends):
+        @pl.when(sends)
+        def _():
+            back_copy(hop, place, where).start()
+
+    for hop in (3, 4, 1, 2, 0):
         keys = pairs[hop, :, :head]
         exps = weights[hop]
         probs_back = matrix_product(pairs[hop, :, head:], grad_cols)
@@ -357,30 +427,37 @@
         keys_back = matrix_product(scores_back, query_rows)
         values_back = matrix_product(exps, grad_rows)
         query_back = query_back + matrix_product(keys.astype(f32).T.astype(bf16), scores_back)
-        if hop > 0:
-            pair_grads[hop - 1, :, :head] = keys_back.astype(bf16)
-            pair_grads[hop - 1, :, head:] = values_back.astype(bf16)
-
-            @pl.when(ctx >= hop)
-            def _(hop=hop):
-                back_copy(hop).start()
-
-        else:
-            own_keys, own_values = keys_back, values_back
+        pair_back = jnp.concatenate([keys_back, values_back], axis=1)
+        if hop == 3:
+            pair_grads[2] = pair_back.astype(bf16)
+            send_back(3, 0, partner, sends[0])
+        if hop == 4:
+            receive_back(0)
+            pair_back = pair_back + odd_share * pair_recv[0].astype(f32)
+            pair_grads[3] = pair_back.astype(bf16)
+            send_back(4, 1, below, sends[1])
+        if hop == 1:
+            pair_grads[0] = pair_back.astype(bf16)
+            send_back(1, 2, partner, sends[2])
+        if hop == 2:
+            receive_back(2)
+            receive_back(1)
+            pair_back = pair_back + even_share * pair_recv[0].astype(f32)
+            pair_back = pair_back + odd_share * pair_recv[2].astype(f32)
+            pair_back = pair_back + pair_recv[1].astype(f32)
+            pair_grads[1] = pair_back.astype(bf16)
+            send_back(2, 3, below, sends[3])
+        if hop == 0:
+            own_pair = pair_back + even_share * pair_recv[2].astype(f32)
     query_width = heads * head
     for h in range(heads):
         at = slice(h * head, (h + 1) * head)
         pre_grads[:, at] = norm_back(
             query_pre[:, at], query_gain[...], query_back[:, h * block : (h + 1) * block].T
         ).astype(bf16)
-    for hop in range(1, hops + 1):
-
-        @pl.when(ctx + hop < ctx_size)
-        def _(hop=hop):
-            back_copy(hop).wait_recv()
-
-        own_keys = own_keys + pair_recv[hop - 1, :, :head].astype(f32)
-        own_values = own_values + pair_recv[hop - 1, :, head:].astype(f32)
+    receive_back(3)
+    own_pair = own_pair + pair_recv[3].astype(f32)
+    own_keys, own_values = own_pair[:, :head], own_pair[:, head:]
     key_at = slice(query_width, query_width + head)
     value_at = slice(query_width + head, query_width + 2 * head)
     pre_grads[:, key_at] = norm_back(key_pre[...], key_gain[...], own_keys).astype(bf16)
@@ -407,21 +484,8 @@
             multiply_by_transpose(grads[:, :query_width], query_w[...])
             + multiply_by_transpose(grads[:, key_at], key_w[...])
             + multiply_by_transpose(grads[:, value_at], value_w[...])
-            + multiply_by_transpose(mid_grads[which, : 3 * rank], down_w[...])
-        )
-
-    normed_copies = []
-    for step in range(1, tp_size):
-        normed_send[step - 1] = input_part(rows_of(tp_at(step))).astype(bf16)
-        copy = remote(
-            normed_send.at[step - 1],
-            normed_recv.at[step - 1],
-            normed_sems,
-            step - 1,
-            {"tp": tp_at(step)},
-        )
-        copy.start()
-        normed_copies.append(copy)
+            + matrix_product(mid_grads[which, : 3 * rank], down_w[...])
+        )
 
     slice_width, width = window_of(model, tp_size)
     start = window_start(tp, slice_width, width, model)
@@ -476,6 +540,19 @@
         copy.start()
         sum_copies.append(copy)
 
+    normed_copies = []
+    for step in range(1, tp_size):
+        normed_send[step - 1] = input_part(rows_of(tp_at(step))).astype(bf16)
+        copy = remote(
+            normed_send.at[step - 1],
+            normed_recv.at[step - 1],
+            normed_sems,
+            step - 1,
+            {"tp": tp_at(step)},
+        )
+        copy.start()
+        normed_copies.append(copy)
+
     grad_normed[...] = input_part(mine)
     for copy in sum_copies:
         copy.wait()
@@ -508,19 +585,39 @@
 
     for copy in total_copies:
         copy.wait()
-    for index in range(ctx_size):
-        sums_out[:, index * piece_width : (index + 1) * piece_width] = sums_all[index].astype(f32)
+    sums = jnp.concatenate([sums_all[index].astype(f32) for index in range(ctx_size)], axis=1)
+    offset = tp * slice_width - start
+    share = pltpu.roll(sums[:, :width], lax.rem(width - offset, width), 1)[:, :slice_width]
+    ups = sums[:, width : width + query_width]
+    down_out_rows[...] = share[: 3 * rank]
+    out_up_out[...] = share[3 * rank :]
+    query_up_out[...] = ups[:rank]
+    key_up_out[...] = ups[rank : 2 * rank, :head]
+    value_up_out[...] = ups[rank : 2 * rank, head : 2 * head]
+    out_down_out[...] = ups[2 * rank : 3 * rank]
 
     for hop in range(1, hops + 1):
 
         @pl.when(ctx + hop < ctx_size)
         def _(hop=hop):
             code_copy(hop).wait_send()
-            pair_copy(hop).wait_send()
-
-        @pl.when(ctx >= hop)
-        def _(hop=hop):
-            back_copy(hop).wait_send()
+
+    for target, sent in (
+        (1, even | (ctx >= 2)),
+        (2, has_up),
+        (3, (even & (ctx >= 2)) | (odd & (ctx >= 4))),
+        (4, has_up & (ctx >= 2)),
+    ):
+
+        @pl.when(sent)
+        def _(target=target):
+            pair_copy(0, target, partner).wait_send()
+
+    for place in range(4):
+
+        @pl.when(sends[place])
+        def _(place=place):
+            back_copy(1, place, partner).wait_send()
 
 
 def on_device(
@@ -550,7 +647,6 @@
     rank = adapter_key_up.shape[0]
     ctx_size = lax.axis_size("ctx")
     tp_size = lax.axis_size("tp")
-    tp_index = lax.axis_index("tp")
     reach = WINDOW // block
     hops = min(reach, ctx_size - 1)
     peers = max(tp_size - 1, 1)
@@ -563,16 +659,23 @@
     whole = pl.BlockSpec(memory_space=pltpu.VMEM)
     in_specs = [whole] * 18
     in_specs[3] = pl.BlockSpec(memory_space=pltpu.SMEM)
-    layer_out, grad_in, sums = pl.pallas_call(
+    layer_out, grad_in, down, query, key, value, out_down, out_up = pl.pallas_call(
         kernel,
         out_shape=(
             jax.ShapeDtypeStruct((rows, model), bf16),
             jax.ShapeDtypeStruct((rows, model), bf16),
-            jax.ShapeDtypeStruct((4 * rank, piece_width * ctx_size), f32),
+            jax.ShapeDtypeStruct((3 * rank, slice_width), f32),
+            jax.ShapeDtypeStruct((rank, query_width), f32),
+            jax.ShapeDtypeStruct((rank, head), f32),
+            jax.ShapeDtypeStruct((rank, head), f32),
+            jax.ShapeDtypeStruct((rank, query_width), f32),
+            jax.ShapeDtypeStruct((rank, slice_width), f32),
         ),
         in_specs=in_specs,
-        out_specs=(whole, whole, whole),
+        out_specs=(whole,) * 8,
         scratch_shapes=[
+            pltpu.VMEM((1, model), f32),
+            pltpu.VMEM((1, model), f32),
             pltpu.VMEM((block, model), bf16),
             pltpu.VMEM((hops + 1, 8, block), jnp.int32),
             pltpu.VMEM((hops + 1, block, 2 * head), bf16),
@@ -620,34 +723,22 @@
         output_gradient,
         document_index.reshape(1, block),
         real_token_count,
-        input_norm_gain.reshape(1, model),
+        input_norm_gain,
         query_norm_gain.reshape(1, head),
         key_norm_gain.reshape(1, head),
-        output_norm_gain.reshape(1, model),
+        output_norm_gain,
         query_projection,
         key_projection,
         value_projection,
         output_projection,
-        adapter_down_maps,
+        adapter_down_maps.T,
         adapter_query_up,
         adapter_key_up,
         adapter_value_up,
-        adapter_output_down,
+        adapter_output_down.T,
         adapter_output_up,
     )
-    offset = tp_index * slice_width - window_start(tp_index, slice_width, width, model)
-    share = lax.dynamic_slice_in_dim(sums[:, :width], offset, slice_width, 1)
-    ups = sums[:, width : width + query_width]
-    return (
-        layer_out,
-        grad_in,
-        share[: 3 * rank].T,
-        ups[:rank],
-        ups[rank : 2 * rank, :head],
-        ups[rank : 2 * rank, head : 2 * head],
-        ups[2 * rank : 3 * rank].T,
-        share[3 * rank :],
-    )
+    return layer_out, grad_in, down.T, query, key, value, out_down.T, out_up
 
 
 def solution(mesh):

time: 83.4 us -> 77.4 us (0.928)
  local copies, waits for them, and re-layouts: 13.2 us -> 6.7 us
    slice x3 -> x0, local copies, waits for them, and re-layouts: 3.16 us -> none  [the longest x1 1.32 us: on_device(): ups[rank:2 * rank, head:2 * head]]
    reshape x2 -> x0, local copies, waits for them, and re-layouts: 2.63 us -> none  [the longest x1 1.31 us: on_device(): input_norm_gain.reshape(1, model)]
    transpose x2 -> x0, local copies, waits for them, and re-layouts: 2.19 us -> none  [the longest x1 1.35 us: on_device(): ups[2 * rank:3 * rank]]
    unnamed x8 -> x22, local copies, waits for them, and re-layouts: 5.2 us -> 6.7 us
where the time goes in v2:
time: 77.4 us; the launch traced here: 77.3 us
  Pallas kernels  69.2 us (89%)
  local copies, waits for them, and re-layouts  6.7 us (9%)
  between operations  1.36 us (2%)
    pallas_call x1, Pallas kernels, on_device(): pl.pallas_call(kernel, out_shape=(jax.ShapeDtypeStruct((rows, model), bf1...  69.2 us
    unnamed x22, local copies, waits for them, and re-layouts  6.7 us

profile of v2, /device:TPU:0, one launch (start us, length us, event | category | flops | bytes accessed | tf_op | source)
XLA Modules:
  0.0 77.3 jit_solution(13097244351358336548)
XLA Ops:
  1.3 69.2 %shard_map.233 = (bf16[128,2688]{1,0:T(8,128)(2,1)}, bf16[128,2688]{1,0:T(8,128)(2,1)}, f32[48,1344]{1,0:T(8,128)}, f32[16,256]{1,0:T(8,128)}, f32[16,128]{1,0:T...) custom-call(bf16[128,2688]{1,0:T(8,128)(2,1)} %refs_0_.1, bf16[128,2688]{1,0:T(8,128)(2,1)} %refs_1_.1, ...), custom_call_target="tpu_custom_call" | custom-call | tf_op jit(solution)/shard_map/pallas_call | solution.py:662
  70.5 0.0 copy-start
  70.5 0.0 copy-start.1
  70.5 0.0 copy-start.4
  70.6 0.0 copy-start.6
  70.6 0.0 copy-start.5
  70.6 0.0 copy-start.3
  70.6 0.0 copy-start.2
  70.6 2.1 %copy.35 = bf16[128,2688]{1,0:T(8,128)(2,1)} copy(bf16[128,2688]{1,0:T(8,128)(2,1)} %get-tuple-element.32) | data formatting | bytes 1376256
  72.7 0.0 copy-done
  72.7 0.8 %copy.36 = bf16[128,2688]{1,0:T(8,128)(2,1)} copy(bf16[128,2688]{1,0:T(8,128)(2,1)S(1)} %copy-done) | data formatting | bytes 1376256
  73.5 0.0 copy-done.1
  73.5 0.7 copy.37
  74.2 0.0 copy-done.4
  74.2 0.6 copy.38
  74.8 0.0 copy-done.6
  74.8 0.6 copy.39
  75.4 0.0 copy-done.5
  75.4 0.6 copy.40
  76.0 0.0 copy-done.3
  76.0 0.6 copy.41
  76.6 0.0 copy-done.2
  76.6 0.6 copy.42
Async XLA Ops:
  70.5 2.1 %copy-start = (bf16[128,2688]{1,0:T(8,128)(2,1)S(1)}, bf16[128,2688]{1,0:T(8,128)(2,1)}, u32[]{:S(2)}) copy-start(bf16[128,2688]{1,0:T(8,128)(2,1)} %get-tuple-element.33) | copy-start | bytes 2064388
  70.5 3.0 %copy-start.1 = (f32[48,1344]{1,0:T(8,128)S(1)}, f32[48,1344]{1,0:T(8,128)}, u32[]{:S(2)}) copy-start(f32[48,1344]{1,0:T(8,128)} %get-tuple-element.18) | copy-start | bytes 774148
  70.5 3.7 %copy-start.4 = (f32[16,256]{1,0:T(8,128)S(1)}, f32[16,256]{1,0:T(8,128)}, u32[]{:S(2)}) copy-start(f32[16,256]{1,0:T(8,128)} %get-tuple-element.35) | copy-start | bytes 49156
  70.6 4.3 %copy-start.6 = (f32[16,128]{1,0:T(8,128)S(1)}, f32[16,128]{1,0:T(8,128)}, u32[]{:S(2)}) copy-start(f32[16,128]{1,0:T(8,128)} %get-tuple-element.36) | copy-start | bytes 24580
  70.6 4.9 %copy-start.5 = (f32[16,128]{1,0:T(8,128)S(1)}, f32[16,128]{1,0:T(8,128)}, u32[]{:S(2)}) copy-start(f32[16,128]{1,0:T(8,128)} %get-tuple-element.37) | copy-start | bytes 24580
  70.6 5.5 %copy-start.3 = (f32[16,256]{1,0:T(8,128)S(1)}, f32[16,256]{1,0:T(8,128)}, u32[]{:S(2)}) copy-start(f32[16,256]{1,0:T(8,128)} %get-tuple-element.22) | copy-start | bytes 49156
  70.6 6.1 %copy-start.2 = (f32[16,1344]{1,0:T(8,128)S(1)}, f32[16,1344]{1,0:T(8,128)}, u32[]{:S(2)}) copy-start(f32[16,1344]{1,0:T(8,128)} %get-tuple-element.39) | copy-start | bytes 258052

commit v3 on v2

--- a/solution.py
+++ b/solution.py
@@ -7,7 +7,7 @@
 
 WINDOW = 1024
 LANES = 128
-NORM_ROWS = 16
+NORM_ROWS = 32
 
 epsilon = 1e-06
 adapter_scale = 2.0
@@ -55,6 +55,7 @@
 
 def layer_kernel(
     shapes,
+    staged,
     tokens,
     output_gradient,
     documents,
@@ -124,6 +125,7 @@
 ):
     ctx_size, tp_size, reach, hops = shapes
     rows, model = tokens.shape
+    chunk = min(NORM_ROWS, rows)
     block = documents.shape[1]
     head = key_w.shape[1]
     heads = query_w.shape[1] // head
@@ -166,12 +168,13 @@
     output_gain[...] = output_gain_vec[...].reshape(1, model)
 
     def norm_chunk(index, carry):
-        at = pl.ds(pl.multiple_of(index * NORM_ROWS, NORM_ROWS), NORM_ROWS)
-        to = pl.ds(pl.multiple_of(tp * rows + index * NORM_ROWS, NORM_ROWS), NORM_ROWS)
+        at = pl.ds(pl.multiple_of(index * chunk, chunk), chunk)
+        to = pl.ds(pl.multiple_of(tp * rows + index * chunk, chunk), chunk)
         normed[to, :] = norm_rows(tokens[at, :].astype(f32), input_gain[...]).astype(bf16)
         return carry
 
-    lax.fori_loop(0, rows // NORM_ROWS, norm_chunk, 0)
+    staged[0].wait()
+    lax.fori_loop(0, rows // chunk, norm_chunk, 0)
 
     lane_pos = lax.broadcasted_iota(jnp.int32, (1, block), 1)
     valid_lane = (lane_pos < token_count[0]).astype(f32)
@@ -242,6 +245,8 @@
     for copy in gathers:
         copy.wait()
 
+    for place in (9, 10, 8, 12):
+        staged[place].wait()
     inputs = normed[...]
     middles = multiply_by_transpose(inputs, down_w[...]).astype(bf16)
     mid_pad[...] = jnp.zeros(mid_pad.shape, f32)
@@ -334,6 +339,7 @@
         piece = outputs[:, h * block : (h + 1) * block] * valid_lane
         attended[:, h * head : (h + 1) * head] = piece.T.astype(bf16)
 
+    staged[11].wait()
     mid_send[...] = jnp.zeros(mid_send.shape, bf16)
     out_copies = []
     for step in range(1, tp_size):
@@ -360,8 +366,8 @@
     pre_norm[...] += adapter_scale * matrix_product(mid_out, out_up[...])
 
     def out_chunk(index, carry):
-        at = pl.ds(pl.multiple_of(index * NORM_ROWS, NORM_ROWS), NORM_ROWS)
-        to = pl.ds(pl.multiple_of(tp * rows + index * NORM_ROWS, NORM_ROWS), NORM_ROWS)
+        at = pl.ds(pl.multiple_of(index * chunk, chunk), chunk)
+        to = pl.ds(pl.multiple_of(tp * rows + index * chunk, chunk), chunk)
         held = pre_norm[at, :]
         for step in range(1, tp_size):
             held = held + out_recv[step - 1, at, :].astype(f32)
@@ -371,7 +377,8 @@
         ).astype(bf16)
         return carry
 
-    lax.fori_loop(0, rows // NORM_ROWS, out_chunk, 0)
+    staged[1].wait()
+    lax.fori_loop(0, rows // chunk, out_chunk, 0)
 
     grad_copies = []
     for step in range(1, tp_size):
@@ -572,7 +579,7 @@
         copy.wait()
 
     def in_chunk(index, carry):
-        at = pl.ds(pl.multiple_of(index * NORM_ROWS, NORM_ROWS), NORM_ROWS)
+        at = pl.ds(pl.multiple_of(index * chunk, chunk), chunk)
         incoming = grad_normed[at, :]
         for step in range(1, tp_size):
             incoming = incoming + normed_recv[step - 1, at, :].astype(f32)
@@ -581,7 +588,7 @@
         ).astype(bf16)
         return carry
 
-    lax.fori_loop(0, rows // NORM_ROWS, in_chunk, 0)
+    lax.fori_loop(0, rows // chunk, in_chunk, 0)
 
     for copy in total_copies:
         copy.wait()
@@ -653,27 +660,71 @@
     slice_width, width = window_of(model, tp_size)
     piece_width = -(-(width + query_width) // (LANES * ctx_size)) * LANES
 
+    order = (0, 9, 10, 8, 12, 11, 1)
+    arguments = (
+        tokens,
+        output_gradient,
+        document_index.reshape(1, block),
+        real_token_count,
+        input_norm_gain,
+        query_norm_gain.reshape(1, head),
+        key_norm_gain.reshape(1, head),
+        output_norm_gain,
+        query_projection,
+        key_projection,
+        value_projection,
+        output_projection,
+        adapter_down_maps.T,
+        adapter_query_up,
+        adapter_key_up,
+        adapter_value_up,
+        adapter_output_down.T,
+        adapter_output_up,
+    )
+
     def kernel(*refs):
-        layer_kernel((ctx_size, tp_size, reach, hops), *refs)
+        inputs, results = list(refs[:18]), refs[18:26]
+        buffers, sems, scratch = refs[26 : 26 + len(order)], refs[26 + len(order)], refs[27 + len(order) :]
+        staged = {}
+        for slot, place in enumerate(order):
+            staged[place] = pltpu.make_async_copy(inputs[place], buffers[slot], sems.at[slot])
+            staged[place].start()
+            inputs[place] = buffers[slot]
+        layer_kernel((ctx_size, tp_size, reach, hops), staged, *inputs, *results, *scratch)
+
+    def copy_results(*refs):
+        copies = [
+            pltpu.make_async_copy(refs[place], refs[8 + place], refs[16].at[place])
+            for place in range(8)
+        ]
+        for copy in copies:
+            copy.start()
+        for copy in copies:
+            copy.wait()
 
     whole = pl.BlockSpec(memory_space=pltpu.VMEM)
     in_specs = [whole] * 18
     in_specs[3] = pl.BlockSpec(memory_space=pltpu.SMEM)
-    layer_out, grad_in, down, query, key, value, out_down, out_up = pl.pallas_call(
+    for place in order:
+        in_specs[place] = pl.BlockSpec(memory_space=pl.ANY)
+    out_shape = (
+        jax.ShapeDtypeStruct((rows, model), bf16),
+        jax.ShapeDtypeStruct((rows, model), bf16),
+        jax.ShapeDtypeStruct((3 * rank, slice_width), f32),
+        jax.ShapeDtypeStruct((rank, query_width), f32),
+        jax.ShapeDtypeStruct((rank, head), f32),
+        jax.ShapeDtypeStruct((rank, head), f32),
+        jax.ShapeDtypeStruct((rank, query_width), f32),
+        jax.ShapeDtypeStruct((rank, slice_width), f32),
+    )
+    results = pl.pallas_call(
         kernel,
-        out_shape=(
-            jax.ShapeDtypeStruct((rows, model), bf16),
-            jax.ShapeDtypeStruct((rows, model), bf16),
-            jax.ShapeDtypeStruct((3 * rank, slice_width), f32),
-            jax.ShapeDtypeStruct((rank, query_width), f32),
-            jax.ShapeDtypeStruct((rank, head), f32),
-            jax.ShapeDtypeStruct((rank, head), f32),
-            jax.ShapeDtypeStruct((rank, query_width), f32),
-            jax.ShapeDtypeStruct((rank, slice_width), f32),
-        ),
+        out_shape=out_shape,
         in_specs=in_specs,
         out_specs=(whole,) * 8,
         scratch_shapes=[
+            *[pltpu.VMEM(arguments[place].shape, arguments[place].dtype) for place in order],
+            pltpu.SemaphoreType.DMA((len(order),)),
             pltpu.VMEM((1, model), f32),
             pltpu.VMEM((1, model), f32),
             pltpu.VMEM((block, model), bf16),
@@ -718,26 +769,16 @@
         compiler_params=pltpu.CompilerParams(
             collective_id=0, has_side_effects=True, vmem_limit_bytes=56 * 1024 * 1024
         ),
-    )(
-        tokens,
-        output_gradient,
-        document_index.reshape(1, block),
-        real_token_count,
-        input_norm_gain,
-        query_norm_gain.reshape(1, head),
-        key_norm_gain.reshape(1, head),
-        output_norm_gain,
-        query_projection,
-        key_projection,
-        value_projection,
-        output_projection,
-        adapter_down_maps.T,
-        adapter_query_up,
-        adapter_key_up,
-        adapter_value_up,
-        adapter_output_down.T,
-        adapter_output_up,
-    )
+    )(*arguments)
+    anywhere = pl.BlockSpec(memory_space=pl.ANY)
+    layer_out, grad_in, down, query, key, value, out_down, out_up = pl.pallas_call(
+        copy_results,
+        out_shape=out_shape,
+        in_specs=[anywhere] * 8,
+        out_specs=(anywhere,) * 8,
+        scratch_shapes=[pltpu.SemaphoreType.DMA((8,))],
+        compiler_params=pltpu.CompilerParams(vmem_limit_bytes=60 * 1024 * 1024),
+    )(*results)
     return layer_out, grad_in, down.T, query, key, value, out_down.T, out_up
 
 

time: 77.4 us -> 124 us (1.60)
  Pallas kernels: 69.2 us -> 122 us
  local copies, waits for them, and re-layouts: 6.7 us -> 0 us
    pallas_call x1 -> x2, Pallas kernels: 69.2 us -> 122 us  [the longest x1 66.9 us: on_device(): pl.pallas_call(kernel, out_shape=out_shape, in_specs=in_specs, out_specs=...]
    unnamed x22 -> x0, local copies, waits for them, and re-layouts: 6.7 us -> none
where the time goes in v3:
time: 124 us; the launch traced here: 123 us
  Pallas kernels  122 us (98%)
  between operations  1.29 us (1%)
    pallas_call x1, Pallas kernels, on_device(): pl.pallas_call(kernel, out_shape=out_shape, in_specs=in_specs, out_specs=...  66.9 us
    pallas_call x1, Pallas kernels, on_device(): pl.pallas_call(copy_results, out_shape=out_shape, in_specs=[anywhere] * 8...  55.3 us

profile of v3, /device:TPU:0, one launch (start us, length us, event | category | flops | bytes accessed | tf_op | source)
XLA Modules:
  0.0 123.4 jit_solution(11003571328282558494)
XLA Ops:
  1.3 66.9 %shard_map.233 = (bf16[128,2688]{1,0:T(8,128)(2,1)}, bf16[128,2688]{1,0:T(8,128)(2,1)}, f32[48,1344]{1,0:T(8,128)}, f32[16,256]{1,0:T(8,128)}, f32[16,128]{1,0:T...) custom-call(bf16[128,2688]{1,0:T(8,128)(2,1)} %refs_0_.1, bf16[128,2688]{1,0:T(8,128)(2,1)} %refs_1_.1, ...), custom_call_target="tpu_custom_call" | custom-call | tf_op jit(solution)/shard_map/pallas_call | solution.py:720
  68.2 55.3 %shard_map.234 = (bf16[128,2688]{1,0:T(8,128)(2,1)}, bf16[128,2688]{1,0:T(8,128)(2,1)}, f32[48,1344]{1,0:T(8,128)}, f32[16,256]{1,0:T(8,128)}, f32[16,128]{1,0:T...) custom-call(bf16[128,2688]{1,0:T(8,128)(2,1)} %get-tuple-element.24.refs_0_, ...), custom_call_target="tpu_custom_call" | custom-call | tf_op jit(solution)/shard_map/pallas_call | solution.py:774

commit v4 on v3

--- a/solution.py
+++ b/solution.py
@@ -693,14 +693,8 @@
         layer_kernel((ctx_size, tp_size, reach, hops), staged, *inputs, *results, *scratch)
 
     def copy_results(*refs):
-        copies = [
-            pltpu.make_async_copy(refs[place], refs[8 + place], refs[16].at[place])
-            for place in range(8)
-        ]
-        for copy in copies:
-            copy.start()
-        for copy in copies:
-            copy.wait()
+        for place in range(8):
+            refs[8 + place][...] = refs[place][...]
 
     whole = pl.BlockSpec(memory_space=pltpu.VMEM)
     in_specs = [whole] * 18
@@ -770,14 +764,11 @@
             collective_id=0, has_side_effects=True, vmem_limit_bytes=56 * 1024 * 1024
         ),
     )(*arguments)
-    anywhere = pl.BlockSpec(memory_space=pl.ANY)
     layer_out, grad_in, down, query, key, value, out_down, out_up = pl.pallas_call(
         copy_results,
         out_shape=out_shape,
-        in_specs=[anywhere] * 8,
-        out_specs=(anywhere,) * 8,
-        scratch_shapes=[pltpu.SemaphoreType.DMA((8,))],
-        compiler_params=pltpu.CompilerParams(vmem_limit_bytes=60 * 1024 * 1024),
+        in_specs=[whole] * 8,
+        out_specs=(whole,) * 8,
     )(*results)
     return layer_out, grad_in, down.T, query, key, value, out_down.T, out_up
 

time: 124 us -> 71.1 us (0.57)
  Pallas kernels: 122 us -> 69.6 us
    pallas_call x1, Pallas kernels: 55.3 us -> 2.71 us  [on_device(): pl.pallas_call(copy_results, out_shape=out_shape, in_specs=[whole] * 8, o...]
where the time goes in v4:
time: 71.1 us; the launch traced here: 70.9 us
  Pallas kernels  69.6 us (98%)
  between operations  1.29 us (2%)
    pallas_call x1, Pallas kernels, on_device(): pl.pallas_call(kernel, out_shape=out_shape, in_specs=in_specs, out_specs=...  66.9 us
    pallas_call x1, Pallas kernels, on_device(): pl.pallas_call(copy_results, out_shape=out_shape, in_specs=[whole] * 8, o...  2.71 us

profile of v4, /device:TPU:0, one launch (start us, length us, event | category | flops | bytes accessed | tf_op | source)
XLA Modules:
  0.0 70.9 jit_solution(8968830897134154523)
XLA Ops:
  1.3 66.9 %shard_map.233 = (bf16[128,2688]{1,0:T(8,128)(2,1)}, bf16[128,2688]{1,0:T(8,128)(2,1)}, f32[48,1344]{1,0:T(8,128)}, f32[16,256]{1,0:T(8,128)}, f32[16,128]{1,0:T...) custom-call(bf16[128,2688]{1,0:T(8,128)(2,1)} %refs_0_.1, bf16[128,2688]{1,0:T(8,128)(2,1)} %refs_1_.1, ...), custom_call_target="tpu_custom_call" | custom-call | tf_op jit(solution)/shard_map/pallas_call | solution.py:714
  68.2 2.7 %shard_map.234 = (bf16[128,2688]{1,0:T(8,128)(2,1)}, bf16[128,2688]{1,0:T(8,128)(2,1)}, f32[48,1344]{1,0:T(8,128)}, f32[16,256]{1,0:T(8,128)}, f32[16,128]{1,0:T...) custom-call(bf16[128,2688]{1,0:T(8,128)(2,1)} %get-tuple-element.24.refs_0_, ...), custom_call_target="tpu_custom_call" | custom-call | tf_op jit(solution)/shard_map/pallas_call | solution.py:767

commit v5 on v4

--- a/solution.py
+++ b/solution.py
@@ -168,7 +168,7 @@
     output_gain[...] = output_gain_vec[...].reshape(1, model)
 
     def norm_chunk(index, carry):
-        at = pl.ds(pl.multiple_of(index * chunk, chunk), chunk)
+        at = pl.ds(index * chunk if isinstance(index, int) else pl.multiple_of(index * chunk, chunk), chunk)
         to = pl.ds(pl.multiple_of(tp * rows + index * chunk, chunk), chunk)
         normed[to, :] = norm_rows(tokens[at, :].astype(f32), input_gain[...]).astype(bf16)
         return carry
@@ -366,7 +366,7 @@
     pre_norm[...] += adapter_scale * matrix_product(mid_out, out_up[...])
 
     def out_chunk(index, carry):
-        at = pl.ds(pl.multiple_of(index * chunk, chunk), chunk)
+        at = pl.ds(index * chunk if isinstance(index, int) else pl.multiple_of(index * chunk, chunk), chunk)
         to = pl.ds(pl.multiple_of(tp * rows + index * chunk, chunk), chunk)
         held = pre_norm[at, :]
         for step in range(1, tp_size):
@@ -378,15 +378,21 @@
         return carry
 
     staged[1].wait()
-    lax.fori_loop(0, rows // chunk, out_chunk, 0)
 
     grad_copies = []
-    for step in range(1, tp_size):
-        copy = remote(
-            grad_full.at[mine], grad_full.at[mine], grad_sems, step - 1, {"tp": tp_at(step)}
-        )
-        copy.start()
-        grad_copies.append(copy)
+    for index in range(rows // chunk):
+        out_chunk(index, 0)
+        part = pl.ds(pl.multiple_of(tp * rows + index * chunk, chunk), chunk)
+        for step in range(1, tp_size):
+            copy = remote(
+                grad_full.at[part],
+                grad_full.at[part],
+                grad_sems,
+                index * (tp_size - 1) + step - 1,
+                {"tp": tp_at(step)},
+            )
+            copy.start()
+            grad_copies.append(copy)
     grad_mid_out = adapter_scale * multiply_by_transpose(grad_full[mine, :], out_up[...])
     small_full[mine, :] = jnp.zeros((rows, 2 * LANES), bf16)
     small_full[mine, :rank] = grad_mid_out.astype(bf16)
@@ -579,7 +585,7 @@
         copy.wait()
 
     def in_chunk(index, carry):
-        at = pl.ds(pl.multiple_of(index * chunk, chunk), chunk)
+        at = pl.ds(index * chunk if isinstance(index, int) else pl.multiple_of(index * chunk, chunk), chunk)
         incoming = grad_normed[at, :]
         for step in range(1, tp_size):
             incoming = incoming + normed_recv[step - 1, at, :].astype(f32)
@@ -752,7 +758,7 @@
             pltpu.SemaphoreType.DMA((2, hops)),
             pltpu.SemaphoreType.DMA((2, peers)),
             pltpu.SemaphoreType.DMA((2, peers)),
-            pltpu.SemaphoreType.DMA((2, peers)),
+            pltpu.SemaphoreType.DMA((2, peers * (rows // min(NORM_ROWS, rows)))),
             pltpu.SemaphoreType.DMA((2, peers)),
             pltpu.SemaphoreType.DMA((2, hops)),
             pltpu.SemaphoreType.DMA((2, peers)),

time: 71.1 us -> 70.6 us (level)
  no operation moved by 1% of the time
where the time goes in v5:
time: 70.6 us; the launch traced here: 70.4 us
  Pallas kernels  69.1 us (98%)
  between operations  1.29 us (2%)
    pallas_call x1, Pallas kernels, on_device(): pl.pallas_call(kernel, out_shape=out_shape, in_specs=in_specs, out_specs=...  66.4 us
    pallas_call x1, Pallas kernels, on_device(): pl.pallas_call(copy_results, out_shape=out_shape, in_specs=[whole] * 8, o...  2.71 us

profile of v5, /device:TPU:0, one launch (start us, length us, event | category | flops | bytes accessed | tf_op | source)
XLA Modules:
  0.0 70.4 jit_solution(8482039285799537688)
XLA Ops:
  1.3 66.4 %shard_map.233 = (bf16[128,2688]{1,0:T(8,128)(2,1)}, bf16[128,2688]{1,0:T(8,128)(2,1)}, f32[48,1344]{1,0:T(8,128)}, f32[16,256]{1,0:T(8,128)}, f32[16,128]{1,0:T...) custom-call(bf16[128,2688]{1,0:T(8,128)(2,1)} %refs_0_.1, bf16[128,2688]{1,0:T(8,128)(2,1)} %refs_1_.1, ...), custom_call_target="tpu_custom_call" | custom-call | tf_op jit(solution)/shard_map/pallas_call | solution.py:720
  67.7 2.7 %shard_map.234 = (bf16[128,2688]{1,0:T(8,128)(2,1)}, bf16[128,2688]{1,0:T(8,128)(2,1)}, f32[48,1344]{1,0:T(8,128)}, f32[16,256]{1,0:T(8,128)}, f32[16,128]{1,0:T...) custom-call(bf16[128,2688]{1,0:T(8,128)(2,1)} %get-tuple-element.24.refs_0_, ...), custom_call_target="tpu_custom_call" | custom-call | tf_op jit(solution)/shard_map/pallas_call | solution.py:773
